TPU v7x, 32 devices: a whole 2x2x4 slice. The times are simulated.
32 devices in a mesh: blk: 16 (over z, y, core), pb: 2 (over x).
Axes of the slice: x: 2, y: 2, z: 4, core: 2. Of those that a mesh axis runs over, the one named last changes fastest.
Arguments:
- tokens: bfloat16 [8192, 768], P(('blk', 'pb')), may hold values from -6 to 6
- memory: bfloat16 [2048, 768], P(('blk', 'pb')), may hold values from -6 to 6
- self_query: bfloat16 [768, 768], P(('blk', 'pb')), may hold values from -0.3125 to 0.3125
- self_key: bfloat16 [768, 768], P(('blk', 'pb')), may hold values from -0.3125 to 0.3125
- self_value: bfloat16 [768, 768], P(('blk', 'pb')), may hold values from -0.21875 to 0.21875
- self_output: bfloat16 [768, 768], P(('blk', 'pb')), may hold values from -0.625 to 0.625
- cross_query: bfloat16 [768, 768], P(('blk', 'pb')), may hold values from -0.3125 to 0.3125
- cross_key: bfloat16 [768, 768], P(('blk', 'pb')), may hold values from -0.3125 to 0.3125
- cross_value: bfloat16 [768, 768], P(('blk', 'pb')), may hold values from -0.21875 to 0.21875
- cross_output: bfloat16 [768, 768], P(('blk', 'pb')), may hold values from -0.875 to 0.875
- feed_in: bfloat16 [768, 3072], P(('blk', 'pb')), may hold values from -0.21875 to 0.21875
- feed_out: bfloat16 [3072, 768], P(('blk', 'pb')), may hold values from -0.109375 to 0.109375
- gain_self: bfloat16 [768], P(('blk', 'pb')), may hold values from 0.099609375 to 1.8984375
- gain_cross: bfloat16 [768], P(('blk', 'pb')), may hold values from 0.099609375 to 1.8984375
- gain_feed: bfloat16 [768], P(('blk', 'pb')), may hold values from 0.099609375 to 1.8984375
- doc_lengths: int32 [5], replicated, may hold values from 1 to 1024, as said below
- seg_doc: int32 [16], replicated, may hold values from 0 to 4, as said below
- cotangent: bfloat16 [8192, 768], P(('blk', 'pb')), may hold values from -6 to 6
Outputs:
- layer_output: bfloat16 [8192, 768], P(('blk', 'pb'))
- gradient_tokens: float32 [8192, 768], P(('blk', 'pb'))
- gradient_memory: float32 [2048, 768], P(('blk', 'pb'))
- gradient_self_query: float32 [768, 768], P(('blk', 'pb'))
- gradient_self_key: float32 [768, 768], P(('blk', 'pb'))
- gradient_self_value: float32 [768, 768], P(('blk', 'pb'))
- gradient_self_output: float32 [768, 768], P(('blk', 'pb'))
- gradient_cross_query: float32 [768, 768], P(('blk', 'pb'))
- gradient_cross_key: float32 [768, 768], P(('blk', 'pb'))
- gradient_cross_value: float32 [768, 768], P(('blk', 'pb'))
- gradient_cross_output: float32 [768, 768], P(('blk', 'pb'))
- gradient_feed_in: float32 [768, 3072], P(('blk', 'pb'))
- gradient_feed_out: float32 [3072, 768], P(('blk', 'pb'))
- gradient_gain_self: float32 [768], P(('blk', 'pb'))
- gradient_gain_cross: float32 [768], P(('blk', 'pb'))
- gradient_gain_feed: float32 [768], P(('blk', 'pb'))
Inputs may be any that keep to these rules, and one draw needn't show every extreme that they name: `doc_lengths`: the 5 lengths sum to 2048; exactly one of them equals 1024. `seg_doc`: every document is read by at least one segment.
All inputs are finite; a program needn't handle non-finite values.
Results may differ from a plain program's by a relative error of at most 0.03.
The roundings to bfloat16 on the way count: a program that leaves them out, or rounds other values in their place, can miss the bound.
Values may be sent and summed in bfloat16 or wider, within the bound.
No kernel may reach another device: no remote copies, remote signals or barrier semaphores. Data moves between devices by JAX's collectives and lax.ppermute only.
A program may use at most 192 MiB of HBM per device.

v0:
```python
import jax
import jax.numpy as jnp
from jax import lax
from jax.sharding import PartitionSpec as P

D = 768
HEADS = 12
HEAD = 64


big_negative = -1e30
epsilon = 1e-05


def as_sent(value):

    def short(part):
        return part.astype(jnp.bfloat16) if part.dtype == jnp.float32 else part

    return jax.tree.map(short, value)


def passed_along(value, axis, by):
    size = lax.axis_size(axis)
    return lax.ppermute(value, axis, [(i, (i + by) % size) for i in range(size)])


def from_behind(block, axis, distance):
    devices = range(lax.axis_size(axis))
    route = [(i - distance, i) for i in devices if i - distance in devices]
    return lax.ppermute(block, axis, route)


def matmul(left, right):
    return jnp.dot(left, right, preferred_element_type=jnp.float32)


def contract_rows(left, right):
    return lax.dot_general(
        left, right, (((0,), (0,)), ((), ())), preferred_element_type=jnp.float32
    )


def times_transpose(left, right):
    return lax.dot_general(
        left, right, (((1,), (1,)), ((), ())), preferred_element_type=jnp.float32
    )


def layer_norm(values, gain):
    centered = values - jnp.mean(values, axis=-1, keepdims=True)
    variance = jnp.mean(centered * centered, axis=-1, keepdims=True)
    return centered * lax.rsqrt(variance + epsilon) * gain


def exact_gelu(values):
    return jax.nn.gelu(values, approximate=False)


def to_heads(values):
    return values.reshape(values.shape[0], HEADS, HEAD)


def table_entry(table, index):
    places = jnp.arange(table.shape[0], dtype=jnp.int32)
    return jnp.sum(jnp.where(places == index, table, 0))


def row_documents(first_row, count, ends):
    rows = first_row + jnp.arange(count, dtype=jnp.int32)
    return jnp.sum((rows[:, None] >= ends[None, :]).astype(jnp.int32), axis=1)


def unchanged(value):
    return value


def fold_pieces(received, pieces):
    return jnp.sum(
        received.reshape((pieces, received.shape[0] // pieces) + received.shape[1:]), axis=0
    )


def turn_whole(pair):
    return jax.tree.map(
        lambda part, own: part.astype(own.dtype), passed_along(as_sent(pair), "blk", 1), pair
    )


def carry_whole(pair):
    return jax.tree.map(
        lambda part, own: part.astype(own.dtype), passed_along(as_sent(pair), "blk", 1), pair
    )


def per_device(
    tokens,
    memory,
    self_query,
    self_key,
    self_value,
    self_output,
    cross_query,
    cross_key,
    cross_value,
    cross_output,
    feed_in,
    feed_out,
    gain_self,
    gain_cross,
    gain_feed,
    doc_lengths,
    seg_doc,
    cotangent,
):
    (
        self_query,
        self_key,
        self_value,
        self_output,
        cross_query,
        cross_key,
        cross_value,
        cross_output,
        feed_in,
        feed_out,
        gain_self,
        gain_cross,
        gain_feed,
    ) = (
        lax.all_gather(self_query, ("blk", "pb"), axis=0, tiled=True),
        lax.all_gather(self_key, ("blk", "pb"), axis=0, tiled=True),
        lax.all_gather(self_value, ("blk", "pb"), axis=0, tiled=True),
        lax.all_gather(self_output, ("blk", "pb"), axis=0, tiled=True),
        lax.all_gather(cross_query, ("blk", "pb"), axis=0, tiled=True),
        lax.all_gather(cross_key, ("blk", "pb"), axis=0, tiled=True),
        lax.all_gather(cross_value, ("blk", "pb"), axis=0, tiled=True),
        lax.all_gather(cross_output, ("blk", "pb"), axis=0, tiled=True),
        lax.all_gather(feed_in, ("blk", "pb"), axis=0, tiled=True),
        lax.all_gather(feed_out, ("blk", "pb"), axis=0, tiled=True),
        lax.all_gather(gain_self, ("blk", "pb"), axis=0, tiled=True),
        lax.all_gather(gain_cross, ("blk", "pb"), axis=0, tiled=True),
        lax.all_gather(gain_feed, ("blk", "pb"), axis=0, tiled=True),
    )
    gain_self = gain_self.astype(jnp.float32)
    gain_cross = gain_cross.astype(jnp.float32)
    gain_feed = gain_feed.astype(jnp.float32)
    token_rows = tokens.shape[0]
    scale = HEAD ** (-0.5)
    first_half = lax.axis_index("pb") == 0
    queries = matmul(tokens, self_query).astype(jnp.bfloat16)
    keys = matmul(tokens, self_key).astype(jnp.bfloat16)
    values = matmul(tokens, self_value).astype(jnp.bfloat16)
    earlier_keys, earlier_values = from_behind((keys, values), "pb", 1)
    all_keys = to_heads(jnp.concatenate([earlier_keys, keys], axis=0))
    all_values = to_heads(jnp.concatenate([earlier_values, values], axis=0))
    query_heads = to_heads(queries)
    rows = lax.broadcasted_iota(jnp.int32, (token_rows, 2 * token_rows), 0)
    columns = lax.broadcasted_iota(jnp.int32, (token_rows, 2 * token_rows), 1)
    allowed = jnp.where(
        columns < token_rows, jnp.logical_not(first_half), columns - token_rows <= rows
    )

    def self_probs():
        scores = (
            jnp.einsum("qhd,khd->hqk", query_heads, all_keys, preferred_element_type=jnp.float32)
            * scale
        )
        scores = jnp.where(allowed[None], scores, big_negative)
        weights = jnp.exp(scores - jnp.max(scores, axis=-1, keepdims=True))
        return weights / jnp.sum(weights, axis=-1, keepdims=True)

    probs = self_probs()
    self_out = (
        jnp.einsum(
            "hqk,khd->qhd",
            probs.astype(jnp.bfloat16),
            all_values,
            preferred_element_type=jnp.float32,
        )
        .reshape(token_rows, D)
        .astype(jnp.bfloat16)
    )
    mid_self = tokens.astype(jnp.float32) + matmul(self_out, self_output)
    hidden_self, back_self = jax.vjp(layer_norm, mid_self, gain_self)
    hidden_self_low = hidden_self.astype(jnp.bfloat16)
    cross_queries = to_heads(matmul(hidden_self_low, cross_query).astype(jnp.bfloat16))
    local_keys = matmul(memory, cross_key).astype(jnp.bfloat16)
    local_values = matmul(memory, cross_value).astype(jnp.bfloat16)
    flat_keys, flat_values = (
        lax.all_gather(local_keys, "pb", axis=0, tiled=True),
        lax.all_gather(local_values, "pb", axis=0, tiled=True),
    )
    block_keys = to_heads(flat_keys)
    block_values = to_heads(flat_values)
    block_rows = block_keys.shape[0]
    cycle_size = lax.axis_size("blk")
    position = lax.axis_index("blk")
    ends = jnp.cumsum(doc_lengths)
    starts = ends - doc_lengths
    document = table_entry(seg_doc, position)
    doc_start = table_entry(starts, document)
    doc_end = table_entry(ends, document)

    def scored(keys_here, first_row):
        scores = (
            jnp.einsum("qhd,khd->hqk", cross_queries, keys_here, preferred_element_type=jnp.float32)
            * scale
        )
        matching = row_documents(first_row, keys_here.shape[0], ends) == document
        return jnp.where(matching[None, None, :], scores, big_negative)

    def touches(first_row, count):
        return (doc_start < first_row + count) & (doc_end > first_row)

    def absorb(state, pair, first_row):

        def absorb_compute(current):
            peak, total, summed = current
            scores = scored(pair[0], first_row)
            new_peak = jnp.maximum(peak, jnp.max(scores, axis=-1))
            weights = jnp.exp(scores - new_peak[..., None])
            factor = jnp.exp(peak - new_peak)
            total = total * factor + jnp.sum(weights, axis=-1)
            summed = summed * factor[..., None] + jnp.einsum(
                "hqk,khd->hqd",
                weights.astype(jnp.bfloat16),
                pair[1],
                preferred_element_type=jnp.float32,
            )
            return (new_peak, total, summed)

        return lax.cond(touches(first_row, pair[0].shape[0]), absorb_compute, unchanged, state)

    start_state = (
        jnp.full((HEADS, token_rows), big_negative, jnp.float32),
        jnp.zeros((HEADS, token_rows), jnp.float32),
        jnp.zeros((HEADS, token_rows, HEAD), jnp.float32),
    )
    whole = (block_keys, block_values)
    state = absorb(start_state, whole, position * block_rows)

    def forward_turn(turn, carried):
        pair, current = carried
        pair = turn_whole(pair)
        anchor = (position - turn) % cycle_size
        return (pair, absorb(current, pair, anchor * block_rows))

    state = lax.fori_loop(1, cycle_size, forward_turn, (whole, state))[1]
    peak, total, summed = state
    cross_heads = jnp.transpose(summed / total[..., None], (1, 0, 2))
    cross_full = cross_heads.reshape(token_rows, D)
    cross_out = cross_full.astype(jnp.bfloat16)
    log_total = peak + jnp.log(total)
    mid_cross = hidden_self + matmul(cross_out, cross_output)
    hidden_cross, back_cross = jax.vjp(layer_norm, mid_cross, gain_cross)
    hidden_cross_low = hidden_cross.astype(jnp.bfloat16)
    inner = matmul(hidden_cross_low, feed_in)
    activated_full, back_gelu = jax.vjp(exact_gelu, inner)
    activated = activated_full.astype(jnp.bfloat16)
    mid_feed = hidden_cross + matmul(activated, feed_out)
    layer_out, back_feed = jax.vjp(layer_norm, mid_feed, gain_feed)
    gradient_feed_mid, gain_feed_sum = back_feed(cotangent.astype(jnp.float32))
    feed_rounded = gradient_feed_mid.astype(jnp.bfloat16)
    sum_feed_out = contract_rows(activated, feed_rounded)
    gradient_inner = back_gelu(times_transpose(feed_rounded, feed_out))[0].astype(jnp.bfloat16)
    sum_feed_in = contract_rows(hidden_cross_low, gradient_inner)
    gradient_hidden_cross = gradient_feed_mid + times_transpose(gradient_inner, feed_in)
    gradient_cross_mid, gain_cross_sum = back_cross(gradient_hidden_cross)
    cross_rounded = gradient_cross_mid.astype(jnp.bfloat16)
    sum_cross_output = contract_rows(cross_out, cross_rounded)
    outgoing = to_heads(times_transpose(cross_rounded, cross_output).astype(jnp.bfloat16))
    balance = jnp.einsum("qhd,qhd->hq", outgoing.astype(jnp.float32), cross_heads)

    def gradient_step(carried, pair, first_row):

        def gradient_compute(current):
            query_grad, key_grad, value_grad = current
            scores = scored(pair[0], first_row)
            weights = jnp.exp(scores - log_total[..., None])
            value_grad = value_grad + jnp.einsum(
                "hqk,qhd->khd",
                weights.astype(jnp.bfloat16),
                outgoing,
                preferred_element_type=jnp.float32,
            )
            weight_grad = jnp.einsum(
                "qhd,khd->hqk", outgoing, pair[1], preferred_element_type=jnp.float32
            )
            score_grad = (weights * (weight_grad - balance[..., None])).astype(jnp.bfloat16)
            query_grad = (
                query_grad
                + jnp.einsum(
                    "hqk,khd->qhd", score_grad, pair[0], preferred_element_type=jnp.float32
                )
                * scale
            )
            key_grad = (
                key_grad
                + jnp.einsum(
                    "hqk,qhd->khd", score_grad, cross_queries, preferred_element_type=jnp.float32
                )
                * scale
            )
            return (query_grad, key_grad, value_grad)

        return lax.cond(touches(first_row, pair[0].shape[0]), gradient_compute, unchanged, carried)

    query_zero = jnp.zeros((token_rows, HEADS, HEAD), jnp.float32)
    block_zero = jnp.zeros((block_rows, HEADS, HEAD), jnp.float32)
    query_grad, key_grad, value_grad = gradient_step(
        (query_zero, block_zero, block_zero), whole, position * block_rows
    )

    def backward_turn(turn, carried):
        pair, query_now, key_now, value_now = carried
        pair = turn_whole(pair)
        key_now, value_now = carry_whole((key_now, value_now))
        anchor = (position - turn) % cycle_size
        query_now, key_now, value_now = gradient_step(
            (query_now, key_now, value_now), pair, anchor * block_rows
        )
        return (pair, query_now, key_now, value_now)

    _, query_grad, key_grad, value_grad = lax.fori_loop(
        1, cycle_size, backward_turn, (whole, query_grad, key_grad, value_grad)
    )
    key_grad, value_grad = carry_whole((key_grad, value_grad))
    key_sum, value_sum = (
        lax.psum_scatter(
            key_grad.reshape(block_rows, D).astype(jnp.bfloat16),
            "pb",
            scatter_dimension=0,
            tiled=True,
        ).astype(jnp.float32),
        lax.psum_scatter(
            value_grad.reshape(block_rows, D).astype(jnp.bfloat16),
            "pb",
            scatter_dimension=0,
            tiled=True,
        ).astype(jnp.float32),
    )
    memory_key_grad = key_sum.astype(jnp.bfloat16)
    memory_value_grad = value_sum.astype(jnp.bfloat16)
    gradient_memory = times_transpose(memory_key_grad, cross_key) + times_transpose(
        memory_value_grad, cross_value
    )
    sum_cross_key = contract_rows(memory, memory_key_grad)
    sum_cross_value = contract_rows(memory, memory_value_grad)
    cross_query_grad = query_grad.reshape(token_rows, D).astype(jnp.bfloat16)
    sum_cross_query = contract_rows(hidden_self_low, cross_query_grad)
    gradient_hidden_self = gradient_cross_mid + times_transpose(cross_query_grad, cross_query)
    gradient_self_mid, gain_self_sum = back_self(gradient_hidden_self)
    self_rounded = gradient_self_mid.astype(jnp.bfloat16)
    sum_self_output = contract_rows(self_out, self_rounded)
    self_outgoing = to_heads(times_transpose(self_rounded, self_output).astype(jnp.bfloat16))
    probs = self_probs()
    weight_grad = jnp.einsum(
        "qhd,khd->hqk", self_outgoing, all_values, preferred_element_type=jnp.float32
    )
    score_grad = (
        probs * (weight_grad - jnp.sum(probs * weight_grad, axis=-1, keepdims=True))
    ).astype(jnp.bfloat16)
    query_part = (
        (
            jnp.einsum("hqk,khd->qhd", score_grad, all_keys, preferred_element_type=jnp.float32)
            * scale
        )
        .reshape(token_rows, D)
        .astype(jnp.bfloat16)
    )
    key_part = (
        jnp.einsum("hqk,qhd->khd", score_grad, query_heads, preferred_element_type=jnp.float32)
        * scale
    ).reshape(2 * token_rows, D)
    value_part = jnp.einsum(
        "hqk,qhd->khd",
        probs.astype(jnp.bfloat16),
        self_outgoing,
        preferred_element_type=jnp.float32,
    ).reshape(2 * token_rows, D)
    later_key, later_value = (
        from_behind(key_part[:token_rows].astype(jnp.bfloat16), "pb", -1).astype(jnp.float32),
        from_behind(value_part[:token_rows].astype(jnp.bfloat16), "pb", -1).astype(jnp.float32),
    )
    self_key_grad = (key_part[token_rows:] + later_key).astype(jnp.bfloat16)
    self_value_grad = (value_part[token_rows:] + later_value).astype(jnp.bfloat16)
    gradient_tokens = (
        gradient_self_mid
        + times_transpose(query_part, self_query)
        + times_transpose(self_key_grad, self_key)
        + times_transpose(self_value_grad, self_value)
    )
    sum_self_query = contract_rows(tokens, query_part)
    sum_self_key = contract_rows(tokens, self_key_grad)
    sum_self_value = contract_rows(tokens, self_value_grad)
    received = (
        lax.all_to_all(
            sum_self_query.astype(jnp.bfloat16), "blk", split_axis=0, concat_axis=0, tiled=True
        ).astype(sum_self_query.dtype),
        lax.all_to_all(
            sum_self_key.astype(jnp.bfloat16), "blk", split_axis=0, concat_axis=0, tiled=True
        ).astype(sum_self_key.dtype),
        lax.all_to_all(
            sum_self_value.astype(jnp.bfloat16), "blk", split_axis=0, concat_axis=0, tiled=True
        ).astype(sum_self_value.dtype),
        lax.all_to_all(
            sum_self_output.astype(jnp.bfloat16), "blk", split_axis=0, concat_axis=0, tiled=True
        ).astype(sum_self_output.dtype),
        lax.all_to_all(
            sum_cross_query.astype(jnp.bfloat16), "blk", split_axis=0, concat_axis=0, tiled=True
        ).astype(sum_cross_query.dtype),
        lax.all_to_all(
            sum_cross_key.astype(jnp.bfloat16), "blk", split_axis=0, concat_axis=0, tiled=True
        ).astype(sum_cross_key.dtype),
        lax.all_to_all(
            sum_cross_value.astype(jnp.bfloat16), "blk", split_axis=0, concat_axis=0, tiled=True
        ).astype(sum_cross_value.dtype),
        lax.all_to_all(
            sum_cross_output.astype(jnp.bfloat16), "blk", split_axis=0, concat_axis=0, tiled=True
        ).astype(sum_cross_output.dtype),
        lax.all_to_all(
            sum_feed_in.astype(jnp.bfloat16), "blk", split_axis=0, concat_axis=0, tiled=True
        ).astype(sum_feed_in.dtype),
        lax.all_to_all(
            sum_feed_out.astype(jnp.bfloat16), "blk", split_axis=0, concat_axis=0, tiled=True
        ).astype(sum_feed_out.dtype),
        lax.all_to_all(
            gain_self_sum.astype(jnp.bfloat16), "blk", split_axis=0, concat_axis=0, tiled=True
        ).astype(gain_self_sum.dtype),
        lax.all_to_all(
            gain_cross_sum.astype(jnp.bfloat16), "blk", split_axis=0, concat_axis=0, tiled=True
        ).astype(gain_cross_sum.dtype),
        lax.all_to_all(
            gain_feed_sum.astype(jnp.bfloat16), "blk", split_axis=0, concat_axis=0, tiled=True
        ).astype(gain_feed_sum.dtype),
    )
    folded = tuple((fold_pieces(piece, cycle_size) for piece in received))
    (
        total_self_query,
        total_self_key,
        total_self_value,
        total_self_output,
        total_cross_query,
        total_cross_key,
        total_cross_value,
        total_cross_output,
        total_feed_in,
        total_feed_out,
        total_gain_self,
        total_gain_cross,
        total_gain_feed,
    ) = (
        lax.psum_scatter(
            folded[0].astype(jnp.bfloat16), "pb", scatter_dimension=0, tiled=True
        ).astype(jnp.float32),
        lax.psum_scatter(
            folded[1].astype(jnp.bfloat16), "pb", scatter_dimension=0, tiled=True
        ).astype(jnp.float32),
        lax.psum_scatter(
            folded[2].astype(jnp.bfloat16), "pb", scatter_dimension=0, tiled=True
        ).astype(jnp.float32),
        lax.psum_scatter(
            folded[3].astype(jnp.bfloat16), "pb", scatter_dimension=0, tiled=True
        ).astype(jnp.float32),
        lax.psum_scatter(
            folded[4].astype(jnp.bfloat16), "pb", scatter_dimension=0, tiled=True
        ).astype(jnp.float32),
        lax.psum_scatter(
            folded[5].astype(jnp.bfloat16), "pb", scatter_dimension=0, tiled=True
        ).astype(jnp.float32),
        lax.psum_scatter(
            folded[6].astype(jnp.bfloat16), "pb", scatter_dimension=0, tiled=True
        ).astype(jnp.float32),
        lax.psum_scatter(
            folded[7].astype(jnp.bfloat16), "pb", scatter_dimension=0, tiled=True
        ).astype(jnp.float32),
        lax.psum_scatter(
            folded[8].astype(jnp.bfloat16), "pb", scatter_dimension=0, tiled=True
        ).astype(jnp.float32),
        lax.psum_scatter(
            folded[9].astype(jnp.bfloat16), "pb", scatter_dimension=0, tiled=True
        ).astype(jnp.float32),
        lax.psum_scatter(
            folded[10].astype(jnp.bfloat16), "pb", scatter_dimension=0, tiled=True
        ).astype(jnp.float32),
        lax.psum_scatter(
            folded[11].astype(jnp.bfloat16), "pb", scatter_dimension=0, tiled=True
        ).astype(jnp.float32),
        lax.psum_scatter(
            folded[12].astype(jnp.bfloat16), "pb", scatter_dimension=0, tiled=True
        ).astype(jnp.float32),
    )
    return (
        layer_out.astype(jnp.bfloat16),
        gradient_tokens,
        gradient_memory,
        total_self_query,
        total_self_key,
        total_self_value,
        total_self_output,
        total_cross_query,
        total_cross_key,
        total_cross_value,
        total_cross_output,
        total_feed_in,
        total_feed_out,
        total_gain_self,
        total_gain_cross,
        total_gain_feed,
    )


def solution(mesh):
    return jax.shard_map(
        per_device,
        mesh=mesh,
        in_specs=(
            P(("blk", "pb"), None),
            P(("blk", "pb"), None),
            P(("blk", "pb"), None),
            P(("blk", "pb"), None),
            P(("blk", "pb"), None),
            P(("blk", "pb"), None),
            P(("blk", "pb"), None),
            P(("blk", "pb"), None),
            P(("blk", "pb"), None),
            P(("blk", "pb"), None),
            P(("blk", "pb"), None),
            P(("blk", "pb"), None),
            P(("blk", "pb")),
            P(("blk", "pb")),
            P(("blk", "pb")),
            P(),
            P(),
            P(("blk", "pb"), None),
        ),
        out_specs=(
            P(("blk", "pb"), None),
            P(("blk", "pb"), None),
            P(("blk", "pb"), None),
            P(("blk", "pb"), None),
            P(("blk", "pb"), None),
            P(("blk", "pb"), None),
            P(("blk", "pb"), None),
            P(("blk", "pb"), None),
            P(("blk", "pb"), None),
            P(("blk", "pb"), None),
            P(("blk", "pb"), None),
            P(("blk", "pb"), None),
            P(("blk", "pb"), None),
            P(("blk", "pb")),
            P(("blk", "pb")),
            P(("blk", "pb")),
        ),
        check_vma=False,
    )
```

profile of v0, /device:TPU:0, one launch (start us, length us, event | category | flops | bytes accessed | tf_op | source)
XLA Modules:
  0.0 1516.9 jit_solution(12394002832375089094)
XLA Ops:
  16.5 42.0 %all-reduce.6 = (bf16[768]{0:T(1024)(128)(2,1)S(1)}, bf16[768]{0:T(1024)(128)(2,1)S(1)}, bf16[768]{0:T(1024)(128)(2,1)S(1)}) all-reduce(bf16[768]{0:T(1024)(128)(2,1)S(1)} %dynamic-update-slice, bf16[768]{0:T(1024)(128)(2,1)S(1)} %dynamic-update-slice.1, ...), channel_id=1, replica_groups=mesh['blk'=16,'pb'=2] {'blk','pb'}, use_global_device_ids=true, to_apply=%add | all-reduce | flops 2304 | bytes 9216
  73.1 50.9 %all-gather.13.cloned.1.call-done = bf16[768,768]{1,0:T(8,128)(2,1)} async-done(((bf16[24,768]{1,0:T(8,128)(2,1)}), bf16[768,768]{1,0:T(8,128)(2,1)}) %all-gather.13.cloned.1.call-update) | async-done | bytes 1179664 | tf_op jit(solution)/shard_map/all_gather | solution.py:131
  126.1 54.0 %all-gather.11.cloned.1.call-done = bf16[768,768]{1,0:T(8,128)(2,1)} async-done(((bf16[24,768]{1,0:T(8,128)(2,1)}), bf16[768,768]{1,0:T(8,128)(2,1)}) %all-gather.11.cloned.1.call-update) | async-done | bytes 1179664 | tf_op jit(solution)/shard_map/all_gather | solution.py:133
  185.9 50.0 %all-gather.19.cloned.1.call-done = bf16[768,768]{1,0:T(8,128)(2,1)} async-done(((bf16[24,768]{1,0:T(8,128)(2,1)}), bf16[768,768]{1,0:T(8,128)(2,1)}) %all-gather.19.cloned.1.call-update) | async-done | bytes 1179664 | tf_op jit(solution)/shard_map/all_gather | solution.py:136
  244.0 47.8 %all-gather.21.cloned.1.call-done = bf16[768,768]{1,0:T(8,128)(2,1)} async-done(((bf16[24,768]{1,0:T(8,128)(2,1)}), bf16[768,768]{1,0:T(8,128)(2,1)}) %all-gather.21.cloned.1.call-update) | async-done | bytes 1179664 | tf_op jit(solution)/shard_map/all_gather | solution.py:137
  313.5 34.2 %all-gather.17.cloned.1.call-done = bf16[768,768]{1,0:T(8,128)(2,1)} async-done(((bf16[24,768]{1,0:T(8,128)(2,1)}), bf16[768,768]{1,0:T(8,128)(2,1)}) %all-gather.17.cloned.1.call-update) | async-done | bytes 1179664 | tf_op jit(solution)/shard_map/all_gather | solution.py:134
  349.8 53.9 %all-gather.23.cloned.1.call-done = bf16[768,768]{1,0:T(8,128)(2,1)} async-done(((bf16[24,768]{1,0:T(8,128)(2,1)}), bf16[768,768]{1,0:T(8,128)(2,1)}) %all-gather.23.cloned.1.call-update) | async-done | bytes 1179664 | tf_op jit(solution)/shard_map/all_gather | solution.py:135
  407.0 212.7 %while.46 = (s32[]{:T(128)}, bf16[128,12,64]{0,2,1:T(8,128)(2,1)S(1)}, bf16[128,12,64]{0,2,1:T(8,128)(2,1)S(1)}, f32[12,256]{1,0:T(8,128)}, f32[12,256]{1,0:T(8,...) while((s32[]{:T(128)}, ...), condition=%wide.region_19.20_spmd, body=%wide.region_13.19_spmd.sunk | while | flops 103817232 | bytes 9636660 | solution.py:249
  521.1 7.5 collective-permute-done
  568.3 9.1 collective-permute-done
  585.5 10.6 collective-permute-done
  622.9 11.5 multiply_convert_fusion.3
  647.1 289.5 %while.47 = (s32[]{:T(128)}, bf16[128,12,64]{0,2,1:T(8,128)(2,1)}, bf16[128,12,64]{0,2,1:T(8,128)(2,1)S(1)}, f32[256,12,64]{0,2,1:T(8,128)S(1)}, f32[128,12,64]{...) while((s32[]{:T(128)}, bf16[128,12,64]{0,2,1:T(8,128)(2,1)}, ...), condition=%wide.region_35.36_spmd, body=%wide.region_31.35_spmd.sunk | while | flops 255494160 | bytes 19491792 | solution.py:325
  976.9 22.4 %all-to-all-done.7 = bf16[16,48,768]{2,1,0:T(8,128)(2,1)S(1)} async-done(((bf16[16,48,768]{2,1,0:T(8,128)(2,1)}), bf16[16,48,768]{2,1,0:T(8,128)(2,1)S(1)}, u32[]{:S(2)}, u32[]{:S(2)}) %all-to-all-start.7) | async-done | bytes 1179680 | tf_op jit(solution)/shard_map/all_to_all | solution.py:419
  1011.9 20.1 %all-to-all-done.4 = bf16[16,48,768]{2,1,0:T(8,128)(2,1)} async-done(((bf16[16,48,768]{2,1,0:T(8,128)(2,1)}), bf16[16,48,768]{2,1,0:T(8,128)(2,1)}, u32[]{:S(2)}, u32[]{:S(2)}) %all-to-all-start.4) | async-done | bytes 1179680 | tf_op jit(solution)/shard_map/all_to_all | solution.py:410
  1032.0 7.5 all-to-all-start.3
  1049.7 15.0 all-to-all-done.3
  1076.3 11.9 collective-permute-done.8
  1089.8 7.6 all-to-all-done
  1097.4 7.5 all-to-all-start.1
  1110.0 11.6 collective-permute-done.9
  1138.2 26.6 %collective-permute-done.10 = bf16[128,12,64]{0,2,1:T(8,128)(2,1)S(1)} collective-permute-done((bf16[128,12,64]{0,2,1:T(8,128)(2,1)S(1)}, bf16[128,12,64]{0,2,1:T(8,128)(2,1)S(1)}, u32[]{:S(2)}, u32[]{:S(2)}) %collective-permute-start.10) | collective-permute-done | bytes 196640 | tf_op jit(solution)/shard_map/ppermute | solution.py:25
  1165.7 13.0 reduce-scatter.37.cloned.1.call-done
  1187.4 26.6 %collective-permute-done.11 = bf16[128,12,64]{0,2,1:T(8,128)(2,1)S(1)} collective-permute-done((bf16[128,12,64]{0,2,1:T(8,128)(2,1)S(1)}, bf16[128,12,64]{0,2,1:T(8,128)(2,1)S(1)}, u32[]{:S(2)}, u32[]{:S(2)}) %collective-permute-start.11) | collective-permute-done | bytes 196640 | tf_op jit(solution)/shard_map/ppermute | solution.py:25
  1214.8 12.6 reduce-scatter.39.cloned.1.call-done
  1240.7 20.1 %all-to-all-done.6 = bf16[16,48,768]{2,1,0:T(8,128)(2,1)} async-done(((bf16[16,48,768]{2,1,0:T(8,128)(2,1)}), bf16[16,48,768]{2,1,0:T(8,128)(2,1)}, u32[]{:S(2)}, u32[]{:S(2)}) %all-to-all-start.6) | async-done | bytes 1179680 | tf_op jit(solution)/shard_map/all_to_all | solution.py:416
  1260.8 7.7 all-to-all-start.9
  1273.6 81.7 %all-to-all-done.9 = bf16[16,192,768]{2,1,0:T(8,128)(2,1)} async-done(((bf16[16,192,768]{2,1,0:T(8,128)(2,1)}), bf16[16,192,768]{2,1,0:T(8,128)(2,1)}, u32[]{:S(2)}, u32[]{:S(2)}) %all-to-all-start.9) | async-done | bytes 4718624 | tf_op jit(solution)/shard_map/all_to_all | solution.py:425
  1355.3 21.9 %all-to-all-start.8 = ((bf16[16,48,3072]{2,1,0:T(8,128)(2,1)}), bf16[16,48,3072]{2,1,0:T(8,128)(2,1)}, u32[]{:S(2)}, u32[]{:S(2)}) async-start(bf16[16,48,3072]{2,1,0:T(8,128)(2,1)} %bitcast.177), calls=%async_computation.16 | async-start | bytes 9437184 | tf_op jit(solution)/shard_map/all_to_all | solution.py:422
  1409.1 54.9 %all-to-all-done.8 = bf16[16,48,3072]{2,1,0:T(8,128)(2,1)} async-done(((bf16[16,48,3072]{2,1,0:T(8,128)(2,1)}), bf16[16,48,3072]{2,1,0:T(8,128)(2,1)}, u32[]{:S(2)}, u32[]{:S(2)}) %all-to-all-start.8) | async-done | bytes 4718624 | tf_op jit(solution)/shard_map/all_to_all | solution.py:422
  1484.3 8.7 reduce-scatter.35.cloned.1.call-done
  1494.7 13.2 reduce-scatter.33.cloned.1.call-done
  (822 shorter events, 769.3 us)
Async XLA Ops:
  7.2 60.7 %all-gather.15.cloned.1.call-start = ((), (), s32[]{:S(2)}) async-start(), calls=%async_computation.27 | async-start | bytes 1216512 | tf_op jit(solution)/shard_map/all_gather | solution.py:132
  7.9 116.0 %all-gather.13.cloned.1.call-start = ((), (), s32[]{:S(2)}) async-start(), calls=%async_computation.26 | async-start | bytes 1216512 | tf_op jit(solution)/shard_map/all_gather | solution.py:131
  8.7 171.3 %all-gather.11.cloned.1.call-start = ((), (), s32[]{:S(2)}) async-start(), calls=%async_computation.25 | async-start | bytes 1216512 | tf_op jit(solution)/shard_map/all_gather | solution.py:133
  9.4 226.5 %all-gather.19.cloned.1.call-start = ((), (), s32[]{:S(2)}) async-start(), calls=%async_computation.29 | async-start | bytes 1216512 | tf_op jit(solution)/shard_map/all_gather | solution.py:136
  10.0 281.8 %all-gather.21.cloned.1.call-start = ((), (), s32[]{:S(2)}) async-start(), calls=%async_computation.30 | async-start | bytes 1216512 | tf_op jit(solution)/shard_map/all_gather | solution.py:137
  10.6 337.1 %all-gather.17.cloned.1.call-start = ((), (), s32[]{:S(2)}) async-start(), calls=%async_computation.28 | async-start | bytes 1216512 | tf_op jit(solution)/shard_map/all_gather | solution.py:134
  11.2 392.6 %all-gather.23.cloned.1.call-start = ((), (), s32[]{:S(2)}) async-start(), calls=%async_computation.31 | async-start | bytes 1216512 | tf_op jit(solution)/shard_map/all_gather | solution.py:135
  11.9 607.9 %all-gather.25.cloned.1.call-start = ((), (), s32[]{:S(2)}) async-start(), calls=%async_computation.32 | async-start | bytes 1216512 | tf_op jit(solution)/shard_map/all_gather | solution.py:138
  12.7 610.2 %all-gather.27.cloned.1.call-start = ((), (), s32[]{:S(2)}) async-start(), calls=%async_computation.33 | async-start | bytes 4866048 | tf_op jit(solution)/shard_map/all_gather | solution.py:139
  13.4 621.0 %all-gather.29.cloned.1.call-start = ((), (), s32[]{:S(2)}) async-start(), calls=%async_computation.34 | async-start | bytes 4866048 | tf_op jit(solution)/shard_map/all_gather | solution.py:140
  69.8 231.8 %collective-permute-start.7 = (bf16[256,768]{1,0:T(8,128)(2,1)S(1)}, bf16[256,768]{1,0:T(8,128)(2,1)S(1)}, u32[]{:S(2)}, u32[]{:S(2)}) collective-permute-start(bf16[256,768]{1,0:T(8,128)(2,1)S(1)} %convolution_convert_fusion.13), channel_id=1, source_target_pairs={{0,1},{2,3},{4,5},{6,7},{8,9},{10,11},{12,13},{14,15},{16,17},{18,... | collective-permute-start | bytes 1179656 | tf_op jit(solution)/shard_map/ppermute | solution.py:31
  181.8 120.1 %collective-permute-start.6 = (bf16[256,768]{1,0:T(8,128)(2,1)S(1)}, bf16[256,768]{1,0:T(8,128)(2,1)}, u32[]{:S(2)}, u32[]{:S(2)}) collective-permute-start(bf16[256,768]{1,0:T(8,128)(2,1)S(1)} %convolution_convert_fusion.15), channel_id=1, source_target_pairs={{0,1},{2,3},{4,5},{6,7},{8,9},{10,11},{12,13},{14,15},{16,17},{18,... | collective-permute-start | bytes 1179656 | tf_op jit(solution)/shard_map/ppermute | solution.py:31
  999.3 32.7 %all-to-all-start.4 = ((bf16[16,48,768]{2,1,0:T(8,128)(2,1)}), bf16[16,48,768]{2,1,0:T(8,128)(2,1)}, u32[]{:S(2)}, u32[]{:S(2)}) async-start(bf16[16,48,768]{2,1,0:T(8,128)(2,1)} %bitcast.184), calls=%async_computation.8 | async-start | bytes 2359296 | tf_op jit(solution)/shard_map/all_to_all | solution.py:410
  1032.0 32.7 %all-to-all-start.3 = ((bf16[16,48,768]{2,1,0:T(8,128)(2,1)}), bf16[16,48,768]{2,1,0:T(8,128)(2,1)}, u32[]{:S(2)}, u32[]{:S(2)}) async-start(bf16[16,48,768]{2,1,0:T(8,128)(2,1)} %bitcast.44), calls=%async_computation.6 | async-start | bytes 2359296 | tf_op jit(solution)/shard_map/all_to_all | solution.py:407
  1064.7 32.7 %all-to-all-start = ((bf16[16,48,768]{2,1,0:T(8,128)(2,1)}), bf16[16,48,768]{2,1,0:T(8,128)(2,1)}, u32[]{:S(2)}, u32[]{:S(2)}) async-start(bf16[16,48,768]{2,1,0:T(8,128)(2,1)} %bitcast.186), calls=%async_computation | async-start | bytes 2359296 | tf_op jit(solution)/shard_map/all_to_all | solution.py:398
  1097.4 32.7 %all-to-all-start.1 = ((bf16[16,48,768]{2,1,0:T(8,128)(2,1)}), bf16[16,48,768]{2,1,0:T(8,128)(2,1)}, u32[]{:S(2)}, u32[]{:S(2)}) async-start(bf16[16,48,768]{2,1,0:T(8,128)(2,1)} %bitcast.185), calls=%async_computation.2 | async-start | bytes 2359296 | tf_op jit(solution)/shard_map/all_to_all | solution.py:401
  1130.2 51.0 %all-to-all-start.2 = ((bf16[16,48,768]{2,1,0:T(8,128)(2,1)}), bf16[16,48,768]{2,1,0:T(8,128)(2,1)S(1)}, u32[]{:S(2)}, u32[]{:S(2)}) async-start(bf16[16,48,768]{2,1,0:T(8,128)(2,1)} %bitcast.183), calls=%async_computation.4 | async-start | bytes 2359296 | tf_op jit(solution)/shard_map/all_to_all | solution.py:404
  1137.7 41.1 %reduce-scatter.37.cloned.1.call-start = ((), (), s32[]{:S(2)}) async-start(), calls=%async_computation.45 | async-start | bytes 294912
  1181.1 48.8 %all-to-all-start.5 = ((bf16[16,48,768]{2,1,0:T(8,128)(2,1)}), bf16[16,48,768]{2,1,0:T(8,128)(2,1)}, u32[]{:S(2)}, u32[]{:S(2)}) async-start(bf16[16,48,768]{2,1,0:T(8,128)(2,1)} %bitcast.180), calls=%async_computation.10 | async-start | bytes 2359296 | tf_op jit(solution)/shard_map/all_to_all | solution.py:413
  1186.8 40.6 %reduce-scatter.39.cloned.1.call-start = ((), (), s32[]{:S(2)}) async-start(), calls=%async_computation.46 | async-start | bytes 294912
  1260.8 94.5 %all-to-all-start.9 = ((bf16[16,192,768]{2,1,0:T(8,128)(2,1)}), bf16[16,192,768]{2,1,0:T(8,128)(2,1)}, u32[]{:S(2)}, u32[]{:S(2)}) async-start(bf16[16,192,768]{2,1,0:T(8,128)(2,1)} %bitcast.176), calls=%async_computation.18 | async-start | bytes 9437184 | tf_op jit(solution)/shard_map/all_to_all | solution.py:425
  1355.3 108.7 %all-to-all-start.8 = ((bf16[16,48,3072]{2,1,0:T(8,128)(2,1)}), bf16[16,48,3072]{2,1,0:T(8,128)(2,1)}, u32[]{:S(2)}, u32[]{:S(2)}) async-start(bf16[16,48,3072]{2,1,0:T(8,128)(2,1)} %bitcast.177), calls=%async_computation.16 | async-start | bytes 9437184 | tf_op jit(solution)/shard_map/all_to_all | solution.py:422
  1377.2 95.9 %reduce-scatter.31.cloned.1.call-start = ((), (), s32[]{:S(2)}) async-start(), calls=%async_computation.42 | async-start | bytes 110592 | tf_op jit(solution)/shard_map/reduce_scatter | solution.py:475
  1378.1 96.4 %reduce-scatter.25.cloned.1.call-start = ((), (), s32[]{:S(2)}) async-start(), calls=%async_computation.39 | async-start | bytes 110592 | tf_op jit(solution)/shard_map/reduce_scatter | solution.py:466
  1380.2 95.6 %reduce-scatter.23.cloned.1.call-start = ((), (), s32[]{:S(2)}) async-start(), calls=%async_computation.38 | async-start | bytes 110592 | tf_op jit(solution)/shard_map/reduce_scatter | solution.py:463
  1382.4 94.9 %reduce-scatter.17.cloned.1.call-start = ((), (), s32[]{:S(2)}) async-start(), calls=%async_computation.35 | async-start | bytes 110592 | tf_op jit(solution)/shard_map/reduce_scatter | solution.py:454
  1384.6 94.1 %reduce-scatter.19.cloned.1.call-start = ((), (), s32[]{:S(2)}) async-start(), calls=%async_computation.36 | async-start | bytes 110592 | tf_op jit(solution)/shard_map/reduce_scatter | solution.py:457
  1386.7 93.4 %reduce-scatter.21.cloned.1.call-start = ((), (), s32[]{:S(2)}) async-start(), calls=%async_computation.37 | async-start | bytes 110592 | tf_op jit(solution)/shard_map/reduce_scatter | solution.py:460
  1388.9 92.6 %reduce-scatter.27.cloned.1.call-start = ((), (), s32[]{:S(2)}) async-start(), calls=%async_computation.40 | async-start | bytes 110592 | tf_op jit(solution)/shard_map/reduce_scatter | solution.py:469
  1391.1 91.9 %reduce-scatter.29.cloned.1.call-start = ((), (), s32[]{:S(2)}) async-start(), calls=%async_computation.41 | async-start | bytes 110592 | tf_op jit(solution)/shard_map/reduce_scatter | solution.py:472
  1393.2 99.8 %reduce-scatter.35.cloned.1.call-start = ((), (), s32[]{:S(2)}) async-start(), calls=%async_computation.44 | async-start | bytes 442368 | tf_op jit(solution)/shard_map/reduce_scatter | solution.py:481
  1398.5 109.5 %reduce-scatter.33.cloned.1.call-start = ((), (), s32[]{:S(2)}) async-start(), calls=%async_computation.43 | async-start | bytes 442368 | tf_op jit(solution)/shard_map/reduce_scatter | solution.py:478
  (161 other events, 2308.3 us)
Sparse Core Ops, SparseCore 0:
  11.0 56.8 all-gather.14
  70.8 53.1 all-gather.12
  126.9 53.0 all-gather.10
  182.8 53.1 all-gather.18
  238.7 53.0 all-gather.20
  294.6 53.0 all-gather.16
  350.6 53.0 all-gather.22
  406.7 56.8 all-gather.24
  466.4 66.8 all-gather.26
  536.2 65.7 all-gather.28
  1165.8 12.8 reduce-scatter.36
  1215.0 12.4 reduce-scatter.38
  1380.8 10.2 reduce-scatter.30
  1393.7 9.9 reduce-scatter.24
  1406.3 9.9 reduce-scatter.22
  1418.9 9.9 reduce-scatter.16
  1431.5 9.9 reduce-scatter.18
  1444.0 9.9 reduce-scatter.20
  1456.2 9.9 reduce-scatter.26
  1468.2 9.9 reduce-scatter.28
  1481.0 12.0 reduce-scatter.34
  1495.8 12.0 reduce-scatter.32
where the time goes:
time: 1510 us; the launch traced here: 1520 us
  waiting for transfers between devices  965 us (64%)
  matrix products  134 us (9%)
  other arithmetic  131 us (9%)
  starting transfers between devices  121 us (8%)
  blocking collectives  58.6 us (4%)
  local copies, waits for them, and re-layouts  47 us (3%)
  loops' own time  42.2 us (3%)
  between operations  17.9 us (1%)
    ppermute x92, waiting for transfers between devices, passed_along(): lax.ppermute(value, axis, [(i, (i + by) % size) for i in range(size)])  349 us
    all_to_all x1, waiting for transfers between devices, per_device(): lax.all_to_all(sum_feed_out.astype(jnp.bfloat16), 'blk', split_axis=0, co...  81.7 us
    all_to_all x1, waiting for transfers between devices, per_device(): lax.all_to_all(sum_feed_in.astype(jnp.bfloat16), 'blk', split_axis=0, con...  54.9 us
    all_gather x1, waiting for transfers between devices, per_device(): lax.all_gather(self_value, ('blk', 'pb'), axis=0, tiled=True)  54 us
    all_gather x1, waiting for transfers between devices, per_device(): lax.all_gather(cross_query, ('blk', 'pb'), axis=0, tiled=True)  53.9 us
    all_gather x1, waiting for transfers between devices, per_device(): lax.all_gather(self_query, ('blk', 'pb'), axis=0, tiled=True)  50.9 us
    all_gather x1, waiting for transfers between devices, per_device(): lax.all_gather(cross_key, ('blk', 'pb'), axis=0, tiled=True)  50 us
    all_gather x1, waiting for transfers between devices, per_device(): lax.all_gather(cross_value, ('blk', 'pb'), axis=0, tiled=True)  47.8 us
  transfers between devices with their start and end apart: 131, of which 116 were waited for; matrix products, arithmetic and copies ran while one was open for 14% of the time, Pallas kernels for 0%

commit v1 on v0

v1 whole, which is shorter than its diff:
```python
import math

import jax
import jax.numpy as jnp
from jax import lax
from jax.experimental import pallas as pl
from jax.experimental.pallas import tpu as pltpu
from jax.sharding import Mesh
from jax.sharding import PartitionSpec as P

D = 768
HEADS = 12
HEAD = 64
PAIR = 2 * HEAD
PAIRS = HEADS // 2
SCALE = HEAD ** (-0.5)

big_negative = -1e30
epsilon = 1e-05
bf16 = jnp.bfloat16
f32 = jnp.float32
ALL = ("z", "y", "c", "x")
VMEM = pl.BlockSpec(memory_space=pltpu.VMEM)
ROOM = 56 * 2**20
SMEM = pl.BlockSpec(memory_space=pltpu.SMEM)


def matmul(left, right):
    return jnp.dot(left, right, preferred_element_type=f32)


def contract_rows(left, right):
    return lax.dot_general(left, right, (((0,), (0,)), ((), ())), preferred_element_type=f32)


def times_transpose(left, right):
    return lax.dot_general(left, right, (((1,), (1,)), ((), ())), preferred_element_type=f32)


def layer_norm(values, gain):
    centered = values - jnp.mean(values, axis=-1, keepdims=True)
    variance = jnp.mean(centered * centered, axis=-1, keepdims=True)
    return centered * lax.rsqrt(variance + epsilon) * gain


def exact_gelu(values):
    return jax.nn.gelu(values, approximate=False)


def table_entry(table, index):
    places = jnp.arange(table.shape[0], dtype=jnp.int32)
    return jnp.sum(jnp.where(places == index, table, 0))


def swapped(value, axis, by=1):
    size = lax.axis_size(axis)
    return lax.ppermute(value, axis, [(i, i ^ by) for i in range(size)])


def position():
    return jnp.stack([lax.axis_index(a).astype(jnp.int32) for a in ALL])


def in_order(pieces, where):
    count = len(pieces)

    def kernel(at, *refs):
        for r in range(count):
            refs[count][jnp.bitwise_xor(at[0], r)] = refs[r][...]

    return pl.pallas_call(
        kernel,
        out_shape=jax.ShapeDtypeStruct((count,) + pieces[0].shape, pieces[0].dtype),
        in_specs=[SMEM] + [VMEM] * count,
        out_specs=VMEM,
        compiler_params=pltpu.CompilerParams(vmem_limit_bytes=ROOM),
        name="in_order",
    )(where, *pieces)


def assembled(planes, cuts, where):
    keys = sorted(planes)
    count, groups, *tail = planes[keys[0]].shape
    tail = tuple(tail)
    n_in = len(keys)

    def kernel(at, *refs):
        for i, (dy, dc, dx) in enumerate(keys):
            y, c, x = (jnp.bitwise_xor(at[1 + j], d) for j, d in enumerate((dy, dc, dx)))
            for o, (first, size) in enumerate(cuts):
                refs[n_in + o][0, y, c, x] = refs[i][0, first : first + size]

    return pl.pallas_call(
        kernel,
        grid=(count,),
        out_shape=[
            jax.ShapeDtypeStruct((count, 2, 2, 2, size) + tail, planes[keys[0]].dtype)
            for _, size in cuts
        ],
        in_specs=[SMEM]
        + [pl.BlockSpec((1, groups) + tail, lambda z: (z, 0, 0, 0)) for _ in range(n_in)],
        out_specs=[
            pl.BlockSpec((1, 2, 2, 2, size) + tail, lambda z: (z, 0, 0, 0, 0, 0, 0))
            for _, size in cuts
        ],
        compiler_params=pltpu.CompilerParams(vmem_limit_bytes=ROOM),
        name="assembled",
    )(where, *(planes[k] for k in keys))


def taken_apart(wholes, where):
    n_in = len(wholes)
    sizes = [w.shape[4] for w in wholes]
    count, tail, dtype = wholes[0].shape[0], wholes[0].shape[5:], wholes[0].dtype

    def kernel(at, *refs):
        for dc in (1, 0):
            for dy in range(2):
                for dx in range(2):
                    y, c, x = (jnp.bitwise_xor(at[1 + j], d) for j, d in enumerate((dy, dc, dx)))
                    first = 0
                    for i in range(n_in):
                        refs[n_in + dc][dy, dx, 0, first : first + sizes[i]] = refs[i][0, y, c, x]
                        first += sizes[i]

    shape = jax.ShapeDtypeStruct((2, 2, count, sum(sizes)) + tail, dtype)
    return pl.pallas_call(
        kernel,
        grid=(count,),
        out_shape=[shape, shape],
        in_specs=[SMEM]
        + [
            pl.BlockSpec((1, 2, 2, 2, size) + tail, lambda z: (z, 0, 0, 0, 0, 0, 0))
            for size in sizes
        ],
        out_specs=[pl.BlockSpec((2, 2, 1, sum(sizes)) + tail, lambda z: (0, 0, z, 0, 0, 0))] * 2,
        compiler_params=pltpu.CompilerParams(vmem_limit_bytes=ROOM),
        name="taken_apart",
    )(where, *wholes)


def gathered(shard, cuts, where, relay):
    pieces = {0: shard}
    by = lax.axis_size("z") // 2
    while by:
        keys = sorted(pieces)
        if len(keys) == 1:
            received = swapped(shard, "z", by)[None]
        else:
            received = swapped(jnp.stack([pieces[k] for k in keys]), "z", by)
        for i, k in enumerate(keys):
            pieces[k ^ by] = received[i]
        by //= 2
    own = in_order([pieces[r] for r in range(len(pieces))], where)
    over_x = swapped(own, "x")
    over_y = swapped(own, "y")
    corner = swapped(over_x, "y") if relay == "y" else swapped(over_y, "x")
    planes = {(0, 0, 0): own, (0, 0, 1): over_x, (1, 0, 0): over_y, (1, 0, 1): corner}
    for dy, _, dx in list(planes):
        planes[dy, 1, dx] = swapped(planes[dy, 0, dx], "c")
    return assembled(planes, cuts, where)


def scattered_sum(wholes, where, relay):
    mine, other = taken_apart(wholes, where)
    received = swapped(other, "c")

    def both(dy, dx):
        return mine[dy, dx].astype(f32) + received[dy, dx].astype(f32)

    corner = swapped(both(1, 1).astype(bf16), relay).astype(f32)
    for_x, for_y = both(0, 1), both(1, 0)
    if relay == "y":
        for_x = for_x + corner
    else:
        for_y = for_y + corner
    total = (
        both(0, 0)
        + swapped(for_x.astype(bf16), "x").astype(f32)
        + swapped(for_y.astype(bf16), "y").astype(f32)
    )
    by = 1
    while by < lax.axis_size("z"):
        halves = total.reshape((total.shape[0] // 2, 2) + total.shape[1:])
        bit = (where[0] // by) % 2
        keep = lax.dynamic_index_in_dim(halves, bit, 1, keepdims=False)
        give = lax.dynamic_index_in_dim(halves, 1 - bit, 1, keepdims=False)
        total = keep + swapped(give.astype(bf16), "z", by).astype(f32)
        by *= 2
    return total[0]


def lane_halves(block):
    lanes = lax.broadcasted_iota(jnp.int32, block.shape, 1)
    zero = jnp.zeros_like(block)
    return jnp.where(lanes < HEAD, block, zero), jnp.where(lanes < HEAD, zero, block)


def allowed_at(shape, first, bounds, causal):
    keys = first + lax.broadcasted_iota(jnp.int32, shape, 0)
    allowed = (keys >= bounds[0]) & (keys < bounds[1])
    if causal:
        queries = lax.broadcasted_iota(jnp.int32, shape, 1)
        allowed = allowed & (keys - shape[1] <= queries)
    return allowed


def attend_kernel(causal, block, bounds, q_ref, k_ref, v_ref, out_ref, low_ref, lse_ref):
    rows, width = q_ref.shape[0], k_ref.shape[0]
    halves = lane_halves(q_ref[...] * SCALE)

    def step(i, state):
        first = pl.multiple_of(i * block, block)
        keys, values = k_ref[pl.ds(first, block)], v_ref[pl.ds(first, block)]
        allowed = allowed_at((block, rows), first, bounds, causal)
        new = []
        for half in range(2):
            peak, total, summed = state[half]
            scores = jnp.where(allowed, times_transpose(keys, halves[half]), big_negative)
            top = jnp.maximum(peak, jnp.max(scores, axis=0, keepdims=True))
            weights = jnp.exp(scores - top)
            factor = jnp.exp(peak - top)
            new.append(
                (
                    top,
                    total * factor + jnp.sum(weights, axis=0, keepdims=True),
                    summed * factor + contract_rows(values, weights.astype(bf16)),
                )
            )
        return tuple(new)

    start = (
        jnp.full((1, rows), big_negative, f32),
        jnp.zeros((1, rows), f32),
        jnp.zeros((PAIR, rows), f32),
    )
    state = (start, start)
    if width == block:
        state = step(0, state)
    else:
        state = lax.fori_loop(0, width // block, step, state)
    outs = [s[2] / s[1] for s in state]
    out = jnp.concatenate([outs[0][:HEAD], outs[1][HEAD:]], axis=0).T
    out_ref[...] = out
    low_ref[...] = out.astype(bf16)
    for half in range(2):
        lse_ref[0, half : half + 1, :] = state[half][0] + jnp.log(state[half][1])


def attend(queries, keys, values, bounds, causal):
    rows, width = queries.shape[0], keys.shape[0]
    block = min(width, 1024)
    spec = lambda n: pl.BlockSpec((n, PAIR), lambda h: (0, h))
    return pl.pallas_call(
        lambda *refs: attend_kernel(causal, block, *refs),
        grid=(PAIRS,),
        in_specs=[SMEM, spec(rows), spec(width), spec(width)],
        out_specs=[spec(rows), spec(rows), pl.BlockSpec((1, 2, rows), lambda h: (h, 0, 0))],
        out_shape=[
            jax.ShapeDtypeStruct((rows, D), f32),
            jax.ShapeDtypeStruct((rows, D), bf16),
            jax.ShapeDtypeStruct((PAIRS, 2, rows), f32),
        ],
        compiler_params=pltpu.CompilerParams(vmem_limit_bytes=48 * 2**20),
        name="attend_self" if causal else "attend_cross",
    )(bounds, queries, keys, values)


def attend_back_kernel(
    causal, block, bounds, q_ref, k_ref, v_ref, o_ref, g_ref, lse_ref, dq_ref, dk_ref, dv_ref
):
    rows, width = q_ref.shape[0], k_ref.shape[0]
    query_halves = lane_halves(q_ref[...] * SCALE)
    grad_halves = lane_halves(g_ref[...])
    products = (g_ref[...].astype(f32) * o_ref[...]).T
    deltas = [
        jnp.sum(products[:HEAD], axis=0, keepdims=True),
        jnp.sum(products[HEAD:], axis=0, keepdims=True),
    ]

    def step(i, state):
        first = pl.multiple_of(i * block, block)
        keys, values = k_ref[pl.ds(first, block)], v_ref[pl.ds(first, block)]
        allowed = allowed_at((block, rows), first, bounds, causal)
        new, key_grad, value_grad = [], None, None
        for half in range(2):
            scores = jnp.where(allowed, times_transpose(keys, query_halves[half]), big_negative)
            probs = jnp.exp(scores - lse_ref[0, half : half + 1, :])
            value_part = matmul(probs.astype(bf16), grad_halves[half])
            slopes = times_transpose(values, grad_halves[half])
            score_grad = (probs * (slopes - deltas[half])).astype(bf16)
            key_part = matmul(score_grad, query_halves[half])
            new.append(state[half] + contract_rows(keys, score_grad))
            key_grad = key_part if key_grad is None else key_grad + key_part
            value_grad = value_part if value_grad is None else value_grad + value_part
        dk_ref[pl.ds(first, block)] = key_grad.astype(bf16)
        dv_ref[pl.ds(first, block)] = value_grad.astype(bf16)
        return tuple(new)

    zero = jnp.zeros((PAIR, rows), f32)
    state = (zero, zero)
    if width == block:
        state = step(0, state)
    else:
        state = lax.fori_loop(0, width // block, step, state)
    dq_ref[...] = (
        (jnp.concatenate([state[0][:HEAD], state[1][HEAD:]], axis=0) * SCALE).T.astype(bf16)
    )


def attend_back(queries, keys, values, out, grad, lse, bounds, causal):
    rows, width = queries.shape[0], keys.shape[0]
    block = min(width, 1024)
    spec = lambda n: pl.BlockSpec((n, PAIR), lambda h: (0, h))
    return pl.pallas_call(
        lambda *refs: attend_back_kernel(causal, block, *refs),
        grid=(PAIRS,),
        in_specs=[SMEM, spec(rows), spec(width), spec(width), spec(rows), spec(rows)]
        + [pl.BlockSpec((1, 2, rows), lambda h: (h, 0, 0))],
        out_specs=[spec(rows), spec(width), spec(width)],
        out_shape=[
            jax.ShapeDtypeStruct((rows, D), bf16),
            jax.ShapeDtypeStruct((width, D), bf16),
            jax.ShapeDtypeStruct((width, D), bf16),
        ],
        compiler_params=pltpu.CompilerParams(vmem_limit_bytes=48 * 2**20),
        name="attend_back_self" if causal else "attend_back_cross",
    )(bounds, queries, keys, values, out, grad, lse)


def padded(shard, rows):
    return jnp.pad(shard, ((0, rows - shard.shape[0]), (0, 0)))


def grouped(shard, group):
    return shard.reshape(shard.shape[0] // group, group, shard.shape[1])


def spread(whole, group):
    z = lax.axis_size("z")
    return whole.reshape(z, 2, 2, 2, whole.shape[0] // (8 * z * group), group, whole.shape[1])


def per_device(
    tokens,
    memory,
    self_query,
    self_key,
    self_value,
    self_output,
    cross_query,
    cross_key,
    cross_value,
    cross_output,
    feed_in,
    feed_out,
    gain_self,
    gain_cross,
    gain_feed,
    doc_lengths,
    seg_doc,
    cotangent,
):
    where = position()
    token_rows = tokens.shape[0]
    count = lax.axis_size("z") * 8
    slots = self_query.shape[0]
    memory_rows = memory.shape[0]
    group = math.gcd(8, slots) if slots % 4 == 0 else slots
    memory_groups = pl.cdiv(memory_rows, group)
    gain_groups = pl.cdiv(3, group)
    gain_rows = gain_groups * group
    slot_groups = slots // group

    earlier = lax.ppermute(tokens, "x", [(0, 1)])

    gains = jnp.pad(jnp.stack([gain_self, gain_cross, gain_feed]), ((0, gain_rows - 3), (0, D - slots)))
    four = [(i * slot_groups, slot_groups) for i in range(4)]
    self_shard = jnp.concatenate(
        [grouped(w, group) for w in (self_query, self_key, self_value, self_output, gains)]
    )
    wholes = gathered(self_shard, four + [(4 * slot_groups, gain_groups)], where, "y")
    self_query, self_key, self_value, self_output = (w.reshape(D, D) for w in wholes[:4])
    gains = wholes[4].reshape(count, gain_rows, D)[:, :3, :slots]
    gain_self, gain_cross, gain_feed = (
        gains[:, i].reshape(D).astype(f32) for i in range(3)
    )
    cross_shard = jnp.concatenate(
        [grouped(w, group) for w in (cross_query, cross_key, cross_value, cross_output)]
        + [grouped(padded(memory, memory_groups * group), group)]
    )
    wholes = gathered(cross_shard, four + [(4 * slot_groups, memory_groups)], where, "x")
    cross_query, cross_key, cross_value, cross_output = (w.reshape(D, D) for w in wholes[:4])
    memory_all = wholes[4].reshape(count, memory_groups * group, D)[:, :memory_rows]
    memory_all = memory_all.reshape(count * memory_rows, D)
    feed_in = gathered(grouped(feed_in, group), [(0, slot_groups)], where, "y")[0].reshape(
        D, feed_in.shape[1]
    )
    feed_out = gathered(grouped(feed_out, group), [(0, feed_out.shape[0] // group)], where, "x")[
        0
    ].reshape(count * feed_out.shape[0], D)

    both_tokens = jnp.concatenate([earlier, tokens], axis=0)
    queries = matmul(tokens, self_query).astype(bf16)
    keys = matmul(both_tokens, self_key).astype(bf16)
    values = matmul(both_tokens, self_value).astype(bf16)
    self_bounds = jnp.stack(
        [jnp.where(where[3] == 0, token_rows, 0), jnp.int32(2 * token_rows)]
    ).astype(jnp.int32)
    self_full, self_out, self_lse = attend(queries, keys, values, self_bounds, True)
    mid_self = tokens.astype(f32) + matmul(self_out, self_output)
    hidden_self, back_self = jax.vjp(layer_norm, mid_self, gain_self)
    hidden_self_low = hidden_self.astype(bf16)

    window = count * memory_rows // 2
    ends = jnp.cumsum(doc_lengths)
    document = table_entry(seg_doc, (where[0] * 2 + where[1]) * 2 + where[2])
    doc_end = table_entry(ends, document)
    doc_start = doc_end - table_entry(doc_lengths, document)
    window_start = jnp.minimum(doc_start, window)
    cross_bounds = jnp.stack([doc_start - window_start, doc_end - window_start]).astype(jnp.int32)
    memory_here = lax.dynamic_slice(memory_all, (window_start, 0), (window, D))
    cross_queries = matmul(hidden_self_low, cross_query).astype(bf16)
    memory_keys = matmul(memory_here, cross_key).astype(bf16)
    memory_values = matmul(memory_here, cross_value).astype(bf16)
    cross_full, cross_out, cross_lse = attend(
        cross_queries, memory_keys, memory_values, cross_bounds, False
    )
    mid_cross = hidden_self + matmul(cross_out, cross_output)
    hidden_cross, back_cross = jax.vjp(layer_norm, mid_cross, gain_cross)
    hidden_cross_low = hidden_cross.astype(bf16)

    inner = matmul(hidden_cross_low, feed_in)
    activated_full, back_gelu = jax.vjp(exact_gelu, inner)
    activated = activated_full.astype(bf16)
    mid_feed = hidden_cross + matmul(activated, feed_out)
    layer_out, back_feed = jax.vjp(layer_norm, mid_feed, gain_feed)
    gradient_feed_mid, gain_feed_sum = back_feed(cotangent.astype(f32))
    feed_rounded = gradient_feed_mid.astype(bf16)
    sum_feed_out = contract_rows(activated, feed_rounded).astype(bf16)
    total_feed_out = scattered_sum([spread(sum_feed_out, group)], where, "y")
    gradient_inner = back_gelu(times_transpose(feed_rounded, feed_out))[0].astype(bf16)
    sum_feed_in = contract_rows(hidden_cross_low, gradient_inner).astype(bf16)
    total_feed_in = scattered_sum([spread(sum_feed_in, group)], where, "x")
    gradient_hidden_cross = gradient_feed_mid + times_transpose(gradient_inner, feed_in)
    gradient_cross_mid, gain_cross_sum = back_cross(gradient_hidden_cross)
    cross_rounded = gradient_cross_mid.astype(bf16)

    sum_cross_output = contract_rows(cross_out, cross_rounded).astype(bf16)
    outgoing = times_transpose(cross_rounded, cross_output).astype(bf16)
    cross_query_grad, memory_key_grad, memory_value_grad = attend_back(
        cross_queries,
        memory_keys,
        memory_values,
        cross_full,
        outgoing,
        cross_lse,
        cross_bounds,
        False,
    )
    sum_cross_key = contract_rows(memory_here, memory_key_grad).astype(bf16)
    sum_cross_value = contract_rows(memory_here, memory_value_grad).astype(bf16)
    sum_cross_query = contract_rows(hidden_self_low, cross_query_grad).astype(bf16)
    sum_memory = lax.dynamic_update_slice(
        jnp.zeros((2 * window, D), bf16),
        (
            times_transpose(memory_key_grad, cross_key)
            + times_transpose(memory_value_grad, cross_value)
        ).astype(bf16),
        (window_start, 0),
    ).reshape(count, memory_rows, D)
    if memory_groups * group > memory_rows:
        sum_memory = jnp.pad(sum_memory, ((0, 0), (0, memory_groups * group - memory_rows), (0, 0)))
    sum_memory = sum_memory.reshape(count * memory_groups * group, D)
    total_cross = scattered_sum(
        [
            spread(s, group)
            for s in (
                sum_cross_query,
                sum_cross_key,
                sum_cross_value,
                sum_cross_output,
                sum_memory,
            )
        ],
        where,
        "y",
    )
    gradient_hidden_self = gradient_cross_mid + times_transpose(cross_query_grad, cross_query)
    gradient_self_mid, gain_self_sum = back_self(gradient_hidden_self)
    self_rounded = gradient_self_mid.astype(bf16)

    sum_self_output = contract_rows(self_out, self_rounded).astype(bf16)
    self_outgoing = times_transpose(self_rounded, self_output).astype(bf16)
    query_grad, key_grad, value_grad = attend_back(
        queries, keys, values, self_full, self_outgoing, self_lse, self_bounds, True
    )
    both_grad = times_transpose(key_grad, self_key) + times_transpose(value_grad, self_value)
    sent_back = lax.ppermute(both_grad[:token_rows].astype(bf16), "x", [(1, 0)])
    sum_self_query = contract_rows(tokens, query_grad).astype(bf16)
    sum_self_key = contract_rows(both_tokens, key_grad).astype(bf16)
    sum_self_value = contract_rows(both_tokens, value_grad).astype(bf16)
    gain_sums = jnp.stack([gain_self_sum, gain_cross_sum, gain_feed_sum]).astype(bf16)
    gain_sums = jnp.pad(
        jnp.transpose(gain_sums.reshape(3, count, slots), (1, 0, 2)),
        ((0, 0), (0, gain_rows - 3), (0, D - slots)),
    ).reshape(count * gain_rows, D)
    total_self = scattered_sum(
        [
            spread(s, group)
            for s in (sum_self_query, sum_self_key, sum_self_value, sum_self_output, gain_sums)
        ],
        where,
        "x",
    )
    gradient_tokens = (
        gradient_self_mid
        + times_transpose(query_grad, self_query)
        + both_grad[token_rows:]
        + sent_back.astype(f32)
    )

    def rows_of(total, first, groups):
        return total[first : first + groups].reshape(groups * group, total.shape[2])

    self_parts = [rows_of(total_self, first, size) for first, size in four]
    cross_parts = [rows_of(total_cross, first, size) for first, size in four]
    gain_parts = rows_of(total_self, 4 * slot_groups, gain_groups)
    return (
        layer_out.astype(bf16),
        gradient_tokens,
        rows_of(total_cross, 4 * slot_groups, memory_groups)[:memory_rows],
        *self_parts,
        *cross_parts,
        rows_of(total_feed_in, 0, total_feed_in.shape[0]),
        rows_of(total_feed_out, 0, total_feed_out.shape[0]),
        gain_parts[0, :slots],
        gain_parts[1, :slots],
        gain_parts[2, :slots],
    )


def solution(mesh):
    fine = Mesh(mesh.devices.reshape(-1, 2, 2, 2), ALL)
    rows = P(ALL, None)
    return jax.shard_map(
        per_device,
        mesh=fine,
        in_specs=(rows,) * 12 + (P(ALL),) * 3 + (P(), P(), rows),
        out_specs=(rows,) * 13 + (P(ALL),) * 3,
        check_vma=False,
    )
```

time: 1510 us -> 466 us (0.31)
  waiting for transfers between devices: 965 us -> 165 us
  other arithmetic: 131 us -> 26.8 us
  Pallas kernels: 0 us -> 94.7 us
  matrix products: 134 us -> 65.7 us
  blocking collectives: 58.6 us -> 0 us
  starting transfers between devices: 121 us -> 70.9 us
  loops' own time: 42.2 us -> 0 us
    all_gather x10 -> x0, waiting for transfers between devices: 294 us -> none  [the longest x1 54 us: per_device(): lax.all_gather(self_value, ('blk', 'pb'), axis=0, tiled=True)]
    all_to_all x13 -> x0, waiting for transfers between devices: 245 us -> none  [the longest x1 81.7 us: per_device(): lax.all_to_all(sum_feed_out.astype(jnp.bfloat16), 'blk', split_axis=0, co...]
    ppermute x96 -> x62, waiting for transfers between devices: 373 us -> 165 us  [the longest x60 165 us: swapped(): return lax.ppermute(value, axis, [(i, i ^ by) for i in range(size)])]
    pallas_call x0 -> x16, Pallas kernels: none -> 94.7 us  [the longest x4 22.7 us: assembled(): pl.pallas_call(kernel, grid=(count,), out_shape=[jax.ShapeDtypeStruct((co...]
    all_to_all x13 -> x0, starting transfers between devices: 92.6 us -> none  [the longest x1 21.9 us: per_device(): lax.all_to_all(sum_feed_in.astype(jnp.bfloat16), 'blk', split_axis=0, con...]
    dot_general x78 -> x10, matrix products: 83.9 us -> 24.8 us  [matmul(): return jnp.dot(left, right, preferred_element_type=f32)]
    convert_element_type x82 -> x11, other arithmetic: 67.6 us -> 11.2 us  [the longest x4 6.16 us: scattered_sum(): for_x.astype(bf16)]
    unnamed x2 -> x0, blocking collectives: 47.3 us -> none
  transfers between devices with their start and end apart: 131 -> 62, of which waited for: 116 -> 23; matrix products, arithmetic and copies ran while one was open for 14% -> 16% of each run, Pallas kernels for 0% -> 12%
where the time goes in v1:
time: 466 us; the launch traced here: 460 us
  waiting for transfers between devices  165 us (35%)
  Pallas kernels  94.7 us (20%)
  starting transfers between devices  70.9 us (15%)
  matrix products  65.7 us (14%)
  local copies, waits for them, and re-layouts  32.6 us (7%)
  other arithmetic  26.8 us (6%)
    ppermute x60, waiting for transfers between devices, swapped(): return lax.ppermute(value, axis, [(i, i ^ by) for i in range(size)])  165 us
    ppermute x60, starting transfers between devices, swapped(): return lax.ppermute(value, axis, [(i, i ^ by) for i in range(size)])  66.2 us
    dot_general x10, matrix products, matmul(): return jnp.dot(left, right, preferred_element_type=f32)  24.8 us
    dot_general x10, matrix products, contract_rows(): lax.dot_general(left, right, (((0,), (0,)), ((), ())), preferred_element_...  24 us
    pallas_call x4, Pallas kernels, assembled(): pl.pallas_call(kernel, grid=(count,), out_shape=[jax.ShapeDtypeStruct((co...  22.7 us
    pallas_call x4, Pallas kernels, taken_apart(): pl.pallas_call(kernel, grid=(count,), out_shape=[shape, shape], in_specs=...  22.7 us
    pallas_call x2, Pallas kernels, attend_back(): pl.pallas_call(lambda *refs: attend_back_kernel(causal, block, *refs), gr...  22.3 us
    pallas_call x2, Pallas kernels, attend(): pl.pallas_call(lambda *refs: attend_kernel(causal, block, *refs), grid=(P...  18.7 us
  transfers between devices with their start and end apart: 62, of which 23 were waited for; matrix products, arithmetic and copies ran while one was open for 16% of the time, Pallas kernels for 12%

profile of v1, /device:TPU:0, one launch (start us, length us, event | category | flops | bytes accessed | tf_op | source)
XLA Modules:
  0.0 460.2 jit_solution(15475603981277609252)
XLA Ops:
  0.6 4.1 collective-permute-start.19
  21.0 4.8 %collective-permute-start.20 = (bf16[2,3,8,3072]{3,2,1,0:T(8,128)(2,1)S(1)}, bf16[2,3,8,3072]{3,2,1,0:T(8,128)(2,1)S(1)}, u32[]{:S(2)}, u32[]{:S(2)}) collective-permute-start(bf16[2,3,8,3072]{3,2,1,0:T(8,128)(2,1)S(1)} %pad_maximum_fusion.2), channel_id=1, source_target_pairs={{0,8},{8,0},{16,24},{24,16},{1,9},{9,1},{17,25},{25,17},{2,10},{10... | collective-permute-start | bytes 884744 | tf_op jit(solution)/shard_map/ppermute | solution.py:57
  25.8 10.0 %collective-permute-done.28.refs_2_ = bf16[12,8,768]{2,1,0:T(8,128)(2,1)S(1)} collective-permute-done((bf16[12,8,768]{2,1,0:T(8,128)(2,1)}, bf16[12,8,768]{2,1,0:T(8,128)(2,1)S(1)}, u32[]{:S(2)}, u32[]{:S(2)}) %collective-permute-start.28) | collective-permute-done | bytes 147488 | tf_op jit(solution)/shard_map/ppermute | solution.py:57
  56.8 8.9 %collective-permute-done.11 = bf16[2,20,8,768]{3,2,1,0:T(8,128)(2,1)S(1)} collective-permute-done((bf16[2,20,8,768]{3,2,1,0:T(8,128)(2,1)S(1)}, bf16[2,20,8,768]{3,2,1,0:T(8,128)(2,1)S(1)}, u32[]{:S(2)}, u32[]{:S(2)}) %collective-permute-start.11) | collective-permute-done | bytes 491552 | tf_op jit(solution)/shard_map/ppermute | solution.py:57
  75.2 9.6 %collective-permute-done.33.refs_4_ = bf16[4,12,8,768]{3,2,1,0:T(8,128)(2,1)S(1)} collective-permute-done((bf16[4,12,8,768]{3,2,1,0:T(8,128)(2,1)}, bf16[4,12,8,768]{3,2,1,0:T(8,128)(2,1)S(1)}, u32[]{:S(2)}, u32[]{:S(2)}) %collective-permute-start.33) | collective-permute-done | bytes 589856 | tf_op jit(solution)/shard_map/ppermute | solution.py:57
  88.4 10.1 %collective-permute-done.5.refs_4_ = bf16[4,13,8,768]{3,2,1,0:T(8,128)(2,1)S(1)} collective-permute-done((bf16[4,13,8,768]{3,2,1,0:T(8,128)(2,1)}, bf16[4,13,8,768]{3,2,1,0:T(8,128)(2,1)S(1)}, u32[]{:S(2)}, u32[]{:S(2)}) %collective-permute-start.5) | collective-permute-done | bytes 639008 | tf_op jit(solution)/shard_map/ppermute | solution.py:57
  99.1 11.8 %collective-permute-done.25.refs_5_ = bf16[4,3,8,3072]{3,2,1,0:T(8,128)(2,1)} collective-permute-done((bf16[4,3,8,3072]{3,2,1,0:T(8,128)(2,1)S(1)}, bf16[4,3,8,3072]{3,2,1,0:T(8,128)(2,1)}, u32[]{:S(2)}, u32[]{:S(2)}) %collective-permute-start.25) | collective-permute-done | bytes 589856 | tf_op jit(solution)/shard_map/ppermute | solution.py:57
  119.2 9.0 %collective-permute-done.6.refs_5_ = bf16[4,13,8,768]{3,2,1,0:T(8,128)(2,1)S(1)} collective-permute-done((bf16[4,13,8,768]{3,2,1,0:T(8,128)(2,1)S(1)}, bf16[4,13,8,768]{3,2,1,0:T(8,128)(2,1)S(1)}, u32[]{:S(2)}, u32[]{:S(2)}) %collective-permute-start.6) | collective-permute-done | bytes 639008 | tf_op jit(solution)/shard_map/ppermute | solution.py:57
  134.2 5.4 %assembled.6 = bf16[4,2,2,2,3,8,3072]{6,5,4,3,2,1,0:T(8,128)(2,1)} custom-call(s32[4]{0:T(128)} %pad_add_fusion.1.at, bf16[4,3,8,3072]{3,2,1,0:T(8,128)(2,1)} %in_order.6.refs_0_, bf16[4,3,8,3072]{3,2,1,0:T(8,128)(2,1)} %copy-done.37, bf16[4,3,8,3072]{3,2,1,0:T(8,128)(2,1)} %collective-permute-done.22.refs_2_, bf16[4,3,8,3072]{3,2,1,0:T(8,128)(2,1)} %copy-done.42, ...), custom_call_target="tpu_custom_call" | custom-call | tf_op jit(solution)/shard_map/assembled/pallas_call | solution.py:93
  139.6 5.1 %assembled.7 = bf16[4,2,2,2,12,8,768]{6,5,4,3,2,1,0:T(8,128)(2,1)} custom-call(s32[4]{0:T(128)} %pad_add_fusion.1.at, bf16[4,12,8,768]{3,2,1,0:T(8,128)(2,1)} %in_order.7.refs_0_, bf16[4,12,8,768]{3,2,1,0:T(8,128)(2,1)} %copy-done.39, bf16[4,12,8,768]{3,2,1,0:T(8,128)(2,1)} %copy-done.40, bf16[4,12,8,768]{3,2,1,0:T(8,128)(2,1)} %copy-done.44, ...), custom_call_target="tpu_custom_call" | custom-call | tf_op jit(solution)/shard_map/assembled/pallas_call | solution.py:93
  150.1 5.3 %assembled.4 = (bf16[4,2,2,2,3,8,768]{6,5,4,3,2,1,0:T(8,128)(2,1)}, bf16[4,2,2,2,3,8,768]{6,5,4,3,2,1,0:T(8,128)(2,1)}, bf16[4,2,2,2,3,8,768]{6,5,4,3,2,1,0:T(8,...) custom-call(s32[4]{0:T(128)} %pad_add_fusion.1.at, ...), custom_call_target="tpu_custom_call" | custom-call | tf_op jit(solution)/shard_map/assembled/pallas_call | solution.py:93
  160.4 10.6 %collective-permute-done.16.refs_5_ = bf16[4,20,8,768]{3,2,1,0:T(8,128)(2,1)} collective-permute-done((bf16[4,20,8,768]{3,2,1,0:T(8,128)(2,1)}, bf16[4,20,8,768]{3,2,1,0:T(8,128)(2,1)}, u32[]{:S(2)}, u32[]{:S(2)}) %collective-permute-start.16) | collective-permute-done | bytes 983072 | tf_op jit(solution)/shard_map/ppermute | solution.py:57
  171.2 7.4 %attend_self.1 = (f32[256,768]{1,0:T(8,128)S(1)}, bf16[256,768]{1,0:T(8,128)(2,1)S(1)}, f32[6,2,256]{2,1,0:T(2,128)S(1)}) custom-call(s32[2]{0:T(128)S(1)} %pad_add_fusion.refs_0_, bf16[256,768]{1,0:T(8,128)(2,1)S(1)} %fusion.12.refs_1_, bf16[512,768]{1,0:T(8,128)(2,1)S(1)} %convolution_convert_fusion.13.refs_2_, ...), custom_call_target="tpu_custom_call" | custom-call | tf_op jit(solution)/shard_map/attend_self/pallas_call | solution.py:254
  180.8 6.9 %assembled.5 = (bf16[4,2,2,2,3,8,768]{6,5,4,3,2,1,0:T(8,128)(2,1)}, bf16[4,2,2,2,3,8,768]{6,5,4,3,2,1,0:T(8,128)(2,1)}, bf16[4,2,2,2,3,8,768]{6,5,4,3,2,1,0:T(8,...) custom-call(s32[4]{0:T(128)} %pad_add_fusion.1.at, ...), custom_call_target="tpu_custom_call" | custom-call | tf_op jit(solution)/shard_map/assembled/pallas_call | solution.py:93
  193.4 11.3 %attend_cross.1 = (f32[256,768]{1,0:T(8,128)S(1)}, bf16[256,768]{1,0:T(8,128)(2,1)S(1)}, f32[6,2,256]{2,1,0:T(2,128)S(1)}) custom-call(s32[2]{0:T(128)S(1)} %pad_add_fusion.2.refs_0_, bf16[256,768]{1,0:T(8,128)(2,1)S(1)} %convolution_convert_fusion.17.refs_1_, bf16[1024,768]{1,0:T(8,128)(2,1)S(1)} %convolution_convert_fusion.3.refs_2_, ...), custom_call_target="tpu_custom_call" | custom-call | tf_op jit(solution)/shard_map/attend_cross/pallas_call | solution.py:254
  207.0 10.8 %multiply_convert_fusion = (bf16[256,3072]{1,0:T(8,128)(2,1)S(1)}, f32[256,3072]{1,0:T(8,128)S(1)}, f32[256,3072]{1,0:T(8,128)}) fusion(bf16[768,3072]{1,0:T(8,128)(2,1)S(1)} %bitcast.258, f32[256,768]{1,0:T(8,128)S(1)} %get-tuple-element.124, f32[768]{0:T(1024)S(1)} %reshape.469, f32[256]{0:T(256)S(1)} %fusion.52, f32[256]{0:T(256)S(1)} %broadcast_multiply_fusion.1), kind=kOutput, calls=%fused_computation.6 | convolution fusion | flops 1259864064 | bytes 13374464 | tf_op jit(solution)/shard_map/dot_general | solution.py:29
  238.6 14.0 %attend_back_cross.1 = (bf16[256,768]{1,0:T(8,128)(2,1)S(1)}, bf16[1024,768]{1,0:T(8,128)(2,1)S(1)}, bf16[1024,768]{1,0:T(8,128)(2,1)S(1)}) custom-call(s32[2]{0:T(128)S(1)} %pad_add_fusion.2.refs_0_, bf16[256,768]{1,0:T(8,128)(2,1)S(1)} %convolution_convert_fusion.17.refs_1_, bf16[1024,768]{1,0:T(8,128)(2,1)} %copy-done, bf16[1024,768]{1,0:T(8,128)(2,1)} %copy-done.1, ...), custom_call_target="tpu_custom_call" | custom-call | tf_op jit(solution)/shard_map/attend_back_cross/pallas_call | solution.py:315
  256.2 8.3 %attend_back_self.1 = (bf16[256,768]{1,0:T(8,128)(2,1)S(1)}, bf16[512,768]{1,0:T(8,128)(2,1)S(1)}, bf16[512,768]{1,0:T(8,128)(2,1)S(1)}) custom-call(s32[2]{0:T(128)S(1)} %pad_add_fusion.refs_0_, bf16[256,768]{1,0:T(8,128)(2,1)S(1)} %fusion.12.refs_1_, bf16[512,768]{1,0:T(8,128)(2,1)S(1)} %convolution_convert_fusion.13.refs_2_, ...), custom_call_target="tpu_custom_call" | custom-call | tf_op jit(solution)/shard_map/attend_back_self/pallas_call | solution.py:315
  269.4 5.1 %taken_apart.6 = (bf16[2,2,4,3,8,3072]{5,4,3,2,1,0:T(8,128)(2,1)}, bf16[2,2,4,3,8,3072]{5,4,3,2,1,0:T(8,128)(2,1)}) custom-call(s32[4]{0:T(128)} %pad_add_fusion.1.at, bf16[4,2,2,2,3,8,3072]{6,5,4,3,2,1,0:T(8,128)(2,1)} %bitcast.246), custom_call_target="tpu_custom_call" | custom-call | tf_op jit(solution)/shard_map/taken_apart/pallas_call | solution.py:127
  276.9 5.1 %taken_apart.7 = (bf16[2,2,4,12,8,768]{5,4,3,2,1,0:T(8,128)(2,1)}, bf16[2,2,4,12,8,768]{5,4,3,2,1,0:T(8,128)(2,1)}) custom-call(s32[4]{0:T(128)} %pad_add_fusion.1.at, bf16[4,2,2,2,12,8,768]{6,5,4,3,2,1,0:T(8,128)(2,1)} %bitcast.245), custom_call_target="tpu_custom_call" | custom-call | tf_op jit(solution)/shard_map/taken_apart/pallas_call | solution.py:127
  290.0 5.3 %taken_apart.5 = (bf16[2,2,4,13,8,768]{5,4,3,2,1,0:T(8,128)(2,1)}, bf16[2,2,4,13,8,768]{5,4,3,2,1,0:T(8,128)(2,1)}) custom-call(s32[4]{0:T(128)} %pad_add_fusion.1.at, bf16[4,2,2,2,3,8,768]{6,5,4,3,2,1,0:T(8,128)(2,1)} %bitcast.269, bf16[4,2,2,2,3,8,768]{6,5,4,3,2,1,0:T(8,128)(2,1)} %bitcast.281, bf16[4,2,2,2,3,8,768]{6,5,4,3,2,1,0:T(8,128)(2,1)} %bitcast.282, ...), custom_call_target="tpu_custom_call" | custom-call | tf_op jit(solution)/shard_map/taken_apart/pallas_call | solution.py:127
  314.4 8.4 %dynamic_update_slice.3 = bf16[2048,768]{1,0:T(8,128)(2,1)} dynamic-update-slice(bf16[2048,768]{1,0:T(8,128)(2,1)} %broadcast_in_dim.63, bf16[1024,768]{1,0:T(8,128)(2,1)} %add_convert_fusion, s32[]{:T(128)S(6)} %select_n.89, s32[]{:T(128)} %constant.176.clone.1) | dynamic-update-slice | bytes 3145732 | tf_op jit(solution)/shard_map/dynamic_update_slice | solution.py:464
  322.7 7.1 %taken_apart.4 = (bf16[2,2,4,20,8,768]{5,4,3,2,1,0:T(8,128)(2,1)}, bf16[2,2,4,20,8,768]{5,4,3,2,1,0:T(8,128)(2,1)}) custom-call(s32[4]{0:T(128)} %pad_add_fusion.1.at, bf16[4,2,2,2,3,8,768]{6,5,4,3,2,1,0:T(8,128)(2,1)} %bitcast.268, bf16[4,2,2,2,3,8,768]{6,5,4,3,2,1,0:T(8,128)(2,1)} %bitcast.279, bf16[4,2,2,2,3,8,768]{6,5,4,3,2,1,0:T(8,128)(2,1)} %bitcast.280, ...), custom_call_target="tpu_custom_call" | custom-call | tf_op jit(solution)/shard_map/taken_apart/pallas_call | solution.py:127
  341.5 6.6 %collective-permute-done.57 = bf16[4,12,8,768]{3,2,1,0:T(8,128)(2,1)S(1)} collective-permute-done((bf16[4,12,8,768]{3,2,1,0:T(8,128)(2,1)S(1)}, bf16[4,12,8,768]{3,2,1,0:T(8,128)(2,1)S(1)}, u32[]{:S(2)}, u32[]{:S(2)}) %collective-permute-start.57) | collective-permute-done | bytes 589856 | tf_op jit(solution)/shard_map/ppermute | solution.py:57
  351.1 8.6 %collective-permute-done.46 = bf16[4,13,8,768]{3,2,1,0:T(8,128)(2,1)S(1)} collective-permute-done((bf16[4,13,8,768]{3,2,1,0:T(8,128)(2,1)S(1)}, bf16[4,13,8,768]{3,2,1,0:T(8,128)(2,1)S(1)}, u32[]{:S(2)}, u32[]{:S(2)}) %collective-permute-start.46) | collective-permute-done | bytes 639008 | tf_op jit(solution)/shard_map/ppermute | solution.py:57
  366.0 7.4 %collective-permute-done.59 = bf16[4,12,8,768]{3,2,1,0:T(8,128)(2,1)S(1)} collective-permute-done((bf16[4,12,8,768]{3,2,1,0:T(8,128)(2,1)S(1)}, bf16[4,12,8,768]{3,2,1,0:T(8,128)(2,1)S(1)}, u32[]{:S(2)}, u32[]{:S(2)}) %collective-permute-start.59) | collective-permute-done | bytes 589856 | tf_op jit(solution)/shard_map/ppermute | solution.py:57
  373.4 14.8 %collective-permute-done.58 = bf16[4,12,8,768]{3,2,1,0:T(8,128)(2,1)S(1)} collective-permute-done((bf16[4,12,8,768]{3,2,1,0:T(8,128)(2,1)S(1)}, bf16[4,12,8,768]{3,2,1,0:T(8,128)(2,1)S(1)}, u32[]{:S(2)}, u32[]{:S(2)}) %collective-permute-start.58) | collective-permute-done | bytes 589856 | tf_op jit(solution)/shard_map/ppermute | solution.py:57
  397.7 6.6 %collective-permute-done.60 = bf16[2,12,8,768]{3,2,1,0:T(8,128)(2,1)S(1)} collective-permute-done((bf16[2,12,8,768]{3,2,1,0:T(8,128)(2,1)S(1)}, bf16[2,12,8,768]{3,2,1,0:T(8,128)(2,1)S(1)}, u32[]{:S(2)}, u32[]{:S(2)}) %collective-permute-start.60) | collective-permute-done | bytes 294944 | tf_op jit(solution)/shard_map/ppermute | solution.py:57
  407.6 10.9 %collective-permute-done.39 = bf16[4,20,8,768]{3,2,1,0:T(8,128)(2,1)S(1)} collective-permute-done((bf16[4,20,8,768]{3,2,1,0:T(8,128)(2,1)S(1)}, bf16[4,20,8,768]{3,2,1,0:T(8,128)(2,1)S(1)}, u32[]{:S(2)}, u32[]{:S(2)}) %collective-permute-start.39) | collective-permute-done | bytes 983072 | tf_op jit(solution)/shard_map/ppermute | solution.py:57
  422.4 14.3 %collective-permute-done.41 = bf16[4,20,8,768]{3,2,1,0:T(8,128)(2,1)S(1)} collective-permute-done((bf16[4,20,8,768]{3,2,1,0:T(8,128)(2,1)S(1)}, bf16[4,20,8,768]{3,2,1,0:T(8,128)(2,1)S(1)}, u32[]{:S(2)}, u32[]{:S(2)}) %collective-permute-start.41) | collective-permute-done | bytes 983072 | tf_op jit(solution)/shard_map/ppermute | solution.py:57
  439.2 9.4 %collective-permute-done.42 = bf16[2,20,8,768]{3,2,1,0:T(8,128)(2,1)S(1)} collective-permute-done((bf16[2,20,8,768]{3,2,1,0:T(8,128)(2,1)S(1)}, bf16[2,20,8,768]{3,2,1,0:T(8,128)(2,1)S(1)}, u32[]{:S(2)}, u32[]{:S(2)}) %collective-permute-start.42) | collective-permute-done | bytes 491552 | tf_op jit(solution)/shard_map/ppermute | solution.py:57
  453.5 5.0 %collective-permute-done.43 = bf16[1,20,8,768]{3,2,1,0:T(8,128)(2,1)S(1)} collective-permute-done((bf16[1,20,8,768]{3,2,1,0:T(8,128)(2,1)S(1)}, bf16[1,20,8,768]{3,2,1,0:T(8,128)(2,1)S(1)}, u32[]{:S(2)}, u32[]{:S(2)}) %collective-permute-start.43) | collective-permute-done | bytes 245792 | tf_op jit(solution)/shard_map/ppermute | solution.py:57
  (376 shorter events, 187.9 us)
Async XLA Ops:
  8.7 30.2 %collective-permute-start.10 = (bf16[20,8,768]{2,1,0:T(8,128)(2,1)S(1)}, bf16[20,8,768]{2,1,0:T(8,128)(2,1)S(1)}, u32[]{:S(2)}, u32[]{:S(2)}) collective-permute-start(bf16[20,8,768]{2,1,0:T(8,128)(2,1)S(1)} %bitcast_dynamic-update-slice_fusion.refs_0_), channel_id=1, source_target_pairs={{0,16},{8,24},{16,0},{24,8},{1,17},{9,25},{17,1},{25,9},{2,18},{10... | collective-permute-start | bytes 737288 | tf_op jit(solution)/shard_map/ppermute | solution.py:57
  12.6 25.0 %collective-permute-start = (bf16[13,8,768]{2,1,0:T(8,128)(2,1)S(1)}, bf16[13,8,768]{2,1,0:T(8,128)(2,1)S(1)}, u32[]{:S(2)}, u32[]{:S(2)}) collective-permute-start(bf16[13,8,768]{2,1,0:T(8,128)(2,1)S(1)} %constant_dynamic-update-slice_fusion.refs_0_), channel_id=1, source_target_pairs={{0,16},{8,24},{16,0},{24,8},{1,17},{9,25},{17,1},{25,9},{2,18},{10... | collective-permute-start | bytes 479240 | tf_op jit(solution)/shard_map/ppermute | solution.py:57
  15.6 30.8 %collective-permute-start.9 = (bf16[256,768]{1,0:T(8,128)(2,1)}, bf16[256,768]{1,0:T(8,128)(2,1)S(1)}, u32[]{:S(2)}, u32[]{:S(2)}) collective-permute-start(bf16[256,768]{1,0:T(8,128)(2,1)} %param.18), channel_id=1, source_target_pairs={{0,1},{2,3},{4,5},{6,7},{8,9},{10,11},{12,13},{14,15},{16,17},{18,... | collective-permute-start | bytes 1179656 | tf_op jit(solution)/shard_map/ppermute | solution.py:375
  39.0 26.7 %collective-permute-start.11 = (bf16[2,20,8,768]{3,2,1,0:T(8,128)(2,1)S(1)}, bf16[2,20,8,768]{3,2,1,0:T(8,128)(2,1)S(1)}, u32[]{:S(2)}, u32[]{:S(2)}) collective-permute-start(bf16[2,20,8,768]{3,2,1,0:T(8,128)(2,1)S(1)} %pad_maximum_fusion), channel_id=1, source_target_pairs={{0,8},{8,0},{16,24},{24,16},{1,9},{9,1},{17,25},{25,17},{2,10},{10... | collective-permute-start | bytes 1474568 | tf_op jit(solution)/shard_map/ppermute | solution.py:57
  46.4 23.7 %collective-permute-start.22 = (bf16[4,3,8,3072]{3,2,1,0:T(8,128)(2,1)}, bf16[4,3,8,3072]{3,2,1,0:T(8,128)(2,1)}, u32[]{:S(2)}, u32[]{:S(2)}) collective-permute-start(bf16[4,3,8,3072]{3,2,1,0:T(8,128)(2,1)} %in_order.6.refs_0_), channel_id=1, source_target_pairs={{0,2},{2,0},{1,3},{3,1},{4,6},{6,4},{5,7},{7,5},{8,10},{10,8},{9,1... | collective-permute-start | bytes 1769480 | tf_op jit(solution)/shard_map/ppermute | solution.py:57
  72.9 25.7 %collective-permute-start.5 = (bf16[4,13,8,768]{3,2,1,0:T(8,128)(2,1)}, bf16[4,13,8,768]{3,2,1,0:T(8,128)(2,1)S(1)}, u32[]{:S(2)}, u32[]{:S(2)}) collective-permute-start(bf16[4,13,8,768]{3,2,1,0:T(8,128)(2,1)} %in_order.4.refs_0_), channel_id=1, source_target_pairs={{0,4},{4,0},{1,5},{5,1},{2,6},{6,2},{3,7},{7,3},{8,12},{12,8},{9,1... | collective-permute-start | bytes 1916936 | tf_op jit(solution)/shard_map/ppermute | solution.py:57
  84.9 26.1 %collective-permute-start.25 = (bf16[4,3,8,3072]{3,2,1,0:T(8,128)(2,1)S(1)}, bf16[4,3,8,3072]{3,2,1,0:T(8,128)(2,1)}, u32[]{:S(2)}, u32[]{:S(2)}) collective-permute-start(bf16[4,3,8,3072]{3,2,1,0:T(8,128)(2,1)S(1)} %collective-permute-done.21.refs_1_), channel_id=1, source_target_pairs={{0,4},{4,0},{1,5},{5,1},{2,6},{6,2},{3,7},{7,3},{8,12},{12,8},{9,1... | collective-permute-start | bytes 1769480 | tf_op jit(solution)/shard_map/ppermute | solution.py:57
  86.8 25.7 %collective-permute-start.26 = (bf16[4,3,8,3072]{3,2,1,0:T(8,128)(2,1)S(1)}, bf16[4,3,8,3072]{3,2,1,0:T(8,128)(2,1)S(1)}, u32[]{:S(2)}, u32[]{:S(2)}) collective-permute-start(bf16[4,3,8,3072]{3,2,1,0:T(8,128)(2,1)S(1)} %collective-permute-done.24.refs_4_), channel_id=1, source_target_pairs={{0,2},{2,0},{1,3},{3,1},{4,6},{6,4},{5,7},{7,5},{8,10},{10,8},{9,1... | collective-permute-start | bytes 1769480 | tf_op jit(solution)/shard_map/ppermute | solution.py:57
  86.9 25.7 %collective-permute-start.34 = (bf16[4,12,8,768]{3,2,1,0:T(8,128)(2,1)S(1)}, bf16[4,12,8,768]{3,2,1,0:T(8,128)(2,1)}, u32[]{:S(2)}, u32[]{:S(2)}) collective-permute-start(bf16[4,12,8,768]{3,2,1,0:T(8,128)(2,1)S(1)} %collective-permute-done.33.refs_4_), channel_id=1, source_target_pairs={{0,1},{1,0},{2,3},{3,2},{4,5},{5,4},{6,7},{7,6},{8,9},{9,8},{10,11... | collective-permute-start | bytes 1769480 | tf_op jit(solution)/shard_map/ppermute | solution.py:57
  116.3 28.4 %collective-permute-start.12 = (bf16[4,20,8,768]{3,2,1,0:T(8,128)(2,1)}, bf16[4,20,8,768]{3,2,1,0:T(8,128)(2,1)}, u32[]{:S(2)}, u32[]{:S(2)}) collective-permute-start(bf16[4,20,8,768]{3,2,1,0:T(8,128)(2,1)} %in_order.5.refs_0_), channel_id=1, source_target_pairs={{0,1},{1,0},{2,3},{3,2},{4,5},{5,4},{6,7},{7,6},{8,9},{9,8},{10,11... | collective-permute-start | bytes 2949128 | tf_op jit(solution)/shard_map/ppermute | solution.py:57
  118.7 29.4 %collective-permute-start.15 = (bf16[4,20,8,768]{3,2,1,0:T(8,128)(2,1)}, bf16[4,20,8,768]{3,2,1,0:T(8,128)(2,1)}, u32[]{:S(2)}, u32[]{:S(2)}) collective-permute-start(bf16[4,20,8,768]{3,2,1,0:T(8,128)(2,1)} %in_order.5.refs_0_), channel_id=1, source_target_pairs={{0,4},{4,0},{1,5},{5,1},{2,6},{6,2},{3,7},{7,3},{8,12},{12,8},{9,1... | collective-permute-start | bytes 2949128 | tf_op jit(solution)/shard_map/ppermute | solution.py:57
  144.7 36.0 %collective-permute-start.13 = (bf16[4,20,8,768]{3,2,1,0:T(8,128)(2,1)}, bf16[4,20,8,768]{3,2,1,0:T(8,128)(2,1)}, u32[]{:S(2)}, u32[]{:S(2)}) collective-permute-start(bf16[4,20,8,768]{3,2,1,0:T(8,128)(2,1)} %in_order.5.refs_0_), channel_id=1, source_target_pairs={{0,2},{2,0},{1,3},{3,1},{4,6},{6,4},{5,7},{7,5},{8,10},{10,8},{9,1... | collective-permute-start | bytes 2949128 | tf_op jit(solution)/shard_map/ppermute | solution.py:57
  149.6 31.1 %collective-permute-start.17 = (bf16[4,20,8,768]{3,2,1,0:T(8,128)(2,1)}, bf16[4,20,8,768]{3,2,1,0:T(8,128)(2,1)}, u32[]{:S(2)}, u32[]{:S(2)}) collective-permute-start(bf16[4,20,8,768]{3,2,1,0:T(8,128)(2,1)} %collective-permute-done.15.refs_4_), channel_id=1, source_target_pairs={{0,2},{2,0},{1,3},{3,1},{4,6},{6,4},{5,7},{7,5},{8,10},{10,8},{9,1... | collective-permute-start | bytes 2949128 | tf_op jit(solution)/shard_map/ppermute | solution.py:57
  149.6 31.1 %collective-permute-start.14 = (bf16[4,20,8,768]{3,2,1,0:T(8,128)(2,1)}, bf16[4,20,8,768]{3,2,1,0:T(8,128)(2,1)}, u32[]{:S(2)}, u32[]{:S(2)}) collective-permute-start(bf16[4,20,8,768]{3,2,1,0:T(8,128)(2,1)} %collective-permute-done.12.refs_1_), channel_id=1, source_target_pairs={{0,2},{2,0},{1,3},{3,1},{4,6},{6,4},{5,7},{7,5},{8,10},{10,8},{9,1... | collective-permute-start | bytes 2949128 | tf_op jit(solution)/shard_map/ppermute | solution.py:57
  268.1 70.4 %collective-permute-start.37 = (bf16[256,768]{1,0:T(8,128)(2,1)}, bf16[256,768]{1,0:T(8,128)(2,1)}, u32[]{:S(2)}, u32[]{:S(2)}) collective-permute-start(bf16[256,768]{1,0:T(8,128)(2,1)} %slice.344), channel_id=1, source_target_pairs={{1,0},{3,2},{5,4},{7,6},{9,8},{11,10},{13,12},{15,14},{17,16},{19,... | collective-permute-start | bytes 1179656 | tf_op jit(solution)/shard_map/ppermute | solution.py:499
  274.5 29.3 %collective-permute-start.50 = (bf16[2,2,4,3,8,3072]{5,4,3,2,1,0:T(8,128)(2,1)}, bf16[2,2,4,3,8,3072]{5,4,3,2,1,0:T(8,128)(2,1)}, u32[]{:S(2)}, u32[]{:S(2)}) collective-permute-start(bf16[2,2,4,3,8,3072]{5,4,3,2,1,0:T(8,128)(2,1)} %get-tuple-element.73), channel_id=1, source_target_pairs={{0,2},{2,0},{1,3},{3,1},{4,6},{6,4},{5,7},{7,5},{8,10},{10,8},{9,1... | collective-permute-start | bytes 7077896 | tf_op jit(solution)/shard_map/ppermute | solution.py:57
  282.1 47.9 %collective-permute-start.56 = (bf16[2,2,4,12,8,768]{5,4,3,2,1,0:T(8,128)(2,1)}, bf16[2,2,4,12,8,768]{5,4,3,2,1,0:T(8,128)(2,1)}, u32[]{:S(2)}, u32[]{:S(2)}) collective-permute-start(bf16[2,2,4,12,8,768]{5,4,3,2,1,0:T(8,128)(2,1)} %get-tuple-element.75), channel_id=1, source_target_pairs={{0,2},{2,0},{1,3},{3,1},{4,6},{6,4},{5,7},{7,5},{8,10},{10,8},{9,1... | collective-permute-start | bytes 7077896 | tf_op jit(solution)/shard_map/ppermute | solution.py:57
  295.3 36.6 %collective-permute-start.44 = (bf16[2,2,4,13,8,768]{5,4,3,2,1,0:T(8,128)(2,1)}, bf16[2,2,4,13,8,768]{5,4,3,2,1,0:T(8,128)(2,1)}, u32[]{:S(2)}, u32[]{:S(2)}) collective-permute-start(bf16[2,2,4,13,8,768]{5,4,3,2,1,0:T(8,128)(2,1)} %get-tuple-element.71), channel_id=1, source_target_pairs={{0,2},{2,0},{1,3},{3,1},{4,6},{6,4},{5,7},{7,5},{8,10},{10,8},{9,1... | collective-permute-start | bytes 7667720 | tf_op jit(solution)/shard_map/ppermute | solution.py:57
  306.8 28.6 %collective-permute-start.52 = (bf16[4,3,8,3072]{3,2,1,0:T(8,128)(2,1)}, bf16[4,3,8,3072]{3,2,1,0:T(8,128)(2,1)}, u32[]{:S(2)}, u32[]{:S(2)}) collective-permute-start(bf16[4,3,8,3072]{3,2,1,0:T(8,128)(2,1)} %get-tuple-element.97), channel_id=1, source_target_pairs={{0,1},{1,0},{2,3},{3,2},{4,5},{5,4},{6,7},{7,6},{8,9},{9,8},{10,11... | collective-permute-start | bytes 1769480 | tf_op jit(solution)/shard_map/ppermute | solution.py:57
  329.9 63.3 %collective-permute-start.38 = (bf16[2,2,4,20,8,768]{5,4,3,2,1,0:T(8,128)(2,1)}, bf16[2,2,4,20,8,768]{5,4,3,2,1,0:T(8,128)(2,1)S(1)}, u32[]{:S(2)}, u32[]{:S(2)}) collective-permute-start(bf16[2,2,4,20,8,768]{5,4,3,2,1,0:T(8,128)(2,1)} %get-tuple-element.69), channel_id=1, source_target_pairs={{0,2},{2,0},{1,3},{3,1},{4,6},{6,4},{5,7},{7,5},{8,10},{10,8},{9,1... | collective-permute-start | bytes 11796488 | tf_op jit(solution)/shard_map/ppermute | solution.py:57
  330.0 31.2 %collective-permute-start.51 = (bf16[4,3,8,3072]{3,2,1,0:T(8,128)(2,1)}, bf16[4,3,8,3072]{3,2,1,0:T(8,128)(2,1)S(1)}, u32[]{:S(2)}, u32[]{:S(2)}) collective-permute-start(bf16[4,3,8,3072]{3,2,1,0:T(8,128)(2,1)} %get-tuple-element.96), channel_id=1, source_target_pairs={{0,1},{1,0},{2,3},{3,2},{4,5},{5,4},{6,7},{7,6},{8,9},{9,8},{10,11... | collective-permute-start | bytes 1769480 | tf_op jit(solution)/shard_map/ppermute | solution.py:57
  335.4 24.3 %collective-permute-start.46 = (bf16[4,13,8,768]{3,2,1,0:T(8,128)(2,1)S(1)}, bf16[4,13,8,768]{3,2,1,0:T(8,128)(2,1)S(1)}, u32[]{:S(2)}, u32[]{:S(2)}) collective-permute-start(bf16[4,13,8,768]{3,2,1,0:T(8,128)(2,1)S(1)} %get-tuple-element.93), channel_id=1, source_target_pairs={{0,1},{1,0},{2,3},{3,2},{4,5},{5,4},{6,7},{7,6},{8,9},{9,8},{10,11... | collective-permute-start | bytes 1916936 | tf_op jit(solution)/shard_map/ppermute | solution.py:57
  338.5 24.6 %collective-permute-start.53 = (bf16[4,3,8,3072]{3,2,1,0:T(8,128)(2,1)S(1)}, bf16[4,3,8,3072]{3,2,1,0:T(8,128)(2,1)S(1)}, u32[]{:S(2)}, u32[]{:S(2)}) collective-permute-start(bf16[4,3,8,3072]{3,2,1,0:T(8,128)(2,1)S(1)} %fusion.15), channel_id=1, source_target_pairs={{0,4},{4,0},{1,5},{5,1},{2,6},{6,2},{3,7},{7,3},{8,12},{12,8},{9,1... | collective-permute-start | bytes 1769480 | tf_op jit(solution)/shard_map/ppermute | solution.py:57
  348.1 25.3 %collective-permute-start.59 = (bf16[4,12,8,768]{3,2,1,0:T(8,128)(2,1)S(1)}, bf16[4,12,8,768]{3,2,1,0:T(8,128)(2,1)S(1)}, u32[]{:S(2)}, u32[]{:S(2)}) collective-permute-start(bf16[4,12,8,768]{3,2,1,0:T(8,128)(2,1)S(1)} %get-tuple-element.95), channel_id=1, source_target_pairs={{0,4},{4,0},{1,5},{5,1},{2,6},{6,2},{3,7},{7,3},{8,12},{12,8},{9,1... | collective-permute-start | bytes 1769480 | tf_op jit(solution)/shard_map/ppermute | solution.py:57
  359.6 30.1 %collective-permute-start.45 = (bf16[4,13,8,768]{3,2,1,0:T(8,128)(2,1)S(1)}, bf16[4,13,8,768]{3,2,1,0:T(8,128)(2,1)S(1)}, u32[]{:S(2)}, u32[]{:S(2)}) collective-permute-start(bf16[4,13,8,768]{3,2,1,0:T(8,128)(2,1)S(1)} %get-tuple-element.92), channel_id=1, source_target_pairs={{0,1},{1,0},{2,3},{3,2},{4,5},{5,4},{6,7},{7,6},{8,9},{9,8},{10,11... | collective-permute-start | bytes 1916936 | tf_op jit(solution)/shard_map/ppermute | solution.py:57
  361.2 27.0 %collective-permute-start.58 = (bf16[4,12,8,768]{3,2,1,0:T(8,128)(2,1)S(1)}, bf16[4,12,8,768]{3,2,1,0:T(8,128)(2,1)S(1)}, u32[]{:S(2)}, u32[]{:S(2)}) collective-permute-start(bf16[4,12,8,768]{3,2,1,0:T(8,128)(2,1)S(1)} %fusion.13), channel_id=1, source_target_pairs={{0,1},{1,0},{2,3},{3,2},{4,5},{5,4},{6,7},{7,6},{8,9},{9,8},{10,11... | collective-permute-start | bytes 1769480 | tf_op jit(solution)/shard_map/ppermute | solution.py:57
  363.1 26.6 %collective-permute-start.47 = (bf16[4,13,8,768]{3,2,1,0:T(8,128)(2,1)S(1)}, bf16[4,13,8,768]{3,2,1,0:T(8,128)(2,1)S(1)}, u32[]{:S(2)}, u32[]{:S(2)}) collective-permute-start(bf16[4,13,8,768]{3,2,1,0:T(8,128)(2,1)S(1)} %fusion.10), channel_id=1, source_target_pairs={{0,4},{4,0},{1,5},{5,1},{2,6},{6,2},{3,7},{7,3},{8,12},{12,8},{9,1... | collective-permute-start | bytes 1916936 | tf_op jit(solution)/shard_map/ppermute | solution.py:57
  391.3 28.8 %collective-permute-start.48 = (bf16[2,13,8,768]{3,2,1,0:T(8,128)(2,1)S(1)}, bf16[2,13,8,768]{3,2,1,0:T(8,128)(2,1)S(1)}, u32[]{:S(2)}, u32[]{:S(2)}) collective-permute-start(bf16[2,13,8,768]{3,2,1,0:T(8,128)(2,1)S(1)} %fusion.34), channel_id=1, source_target_pairs={{0,8},{8,0},{16,24},{24,16},{1,9},{9,1},{17,25},{25,17},{2,10},{10... | collective-permute-start | bytes 958472 | tf_op jit(solution)/shard_map/ppermute | solution.py:57
  393.8 24.8 %collective-permute-start.39 = (bf16[4,20,8,768]{3,2,1,0:T(8,128)(2,1)S(1)}, bf16[4,20,8,768]{3,2,1,0:T(8,128)(2,1)S(1)}, u32[]{:S(2)}, u32[]{:S(2)}) collective-permute-start(bf16[4,20,8,768]{3,2,1,0:T(8,128)(2,1)S(1)} %get-tuple-element.90), channel_id=1, source_target_pairs={{0,4},{4,0},{1,5},{5,1},{2,6},{6,2},{3,7},{7,3},{8,12},{12,8},{9,1... | collective-permute-start | bytes 2949128 | tf_op jit(solution)/shard_map/ppermute | solution.py:57
  395.5 23.9 %collective-permute-start.55 = (bf16[1,3,8,3072]{3,2,1,0:T(8,128)(2,1)S(1)}, bf16[1,3,8,3072]{3,2,1,0:T(8,128)(2,1)S(1)}, u32[]{:S(2)}, u32[]{:S(2)}) collective-permute-start(bf16[1,3,8,3072]{3,2,1,0:T(8,128)(2,1)S(1)} %dynamic-slice_convert_fusion.6), channel_id=1, source_target_pairs={{0,16},{8,24},{16,0},{24,8},{1,17},{9,25},{17,1},{25,9},{2,18},{10... | collective-permute-start | bytes 442376 | tf_op jit(solution)/shard_map/ppermute | solution.py:57
  404.5 34.0 %collective-permute-start.61 = (bf16[1,12,8,768]{3,2,1,0:T(8,128)(2,1)S(1)}, bf16[1,12,8,768]{3,2,1,0:T(8,128)(2,1)S(1)}, u32[]{:S(2)}, u32[]{:S(2)}) collective-permute-start(bf16[1,12,8,768]{3,2,1,0:T(8,128)(2,1)S(1)} %dynamic-slice_convert_fusion.5), channel_id=1, source_target_pairs={{0,16},{8,24},{16,0},{24,8},{1,17},{9,25},{17,1},{25,9},{2,18},{10... | collective-permute-start | bytes 442376 | tf_op jit(solution)/shard_map/ppermute | solution.py:57
  406.1 30.7 %collective-permute-start.41 = (bf16[4,20,8,768]{3,2,1,0:T(8,128)(2,1)S(1)}, bf16[4,20,8,768]{3,2,1,0:T(8,128)(2,1)S(1)}, u32[]{:S(2)}, u32[]{:S(2)}) collective-permute-start(bf16[4,20,8,768]{3,2,1,0:T(8,128)(2,1)S(1)} %get-tuple-element.91), channel_id=1, source_target_pairs={{0,4},{4,0},{1,5},{5,1},{2,6},{6,2},{3,7},{7,3},{8,12},{12,8},{9,1... | collective-permute-start | bytes 2949128 | tf_op jit(solution)/shard_map/ppermute | solution.py:57
  (101 other events, 1645.5 us)

commit v2 on v1

v2 whole, which is shorter than its diff:
```python
import math

import jax
import jax.numpy as jnp
from jax import lax
from jax.experimental import pallas as pl
from jax.experimental.pallas import tpu as pltpu
from jax.sharding import Mesh
from jax.sharding import PartitionSpec as P

D = 768
HEADS = 12
HEAD = 64
PAIR = 2 * HEAD
PAIRS = HEADS // 2
SCALE = HEAD ** (-0.5)

big_negative = -1e30
epsilon = 1e-05
bf16 = jnp.bfloat16
f32 = jnp.float32
ALL = ("z", "y", "c", "x")
NOTHING = pl.CostEstimate(flops=1, bytes_accessed=1, transcendentals=0)
VMEM = pl.BlockSpec(memory_space=pltpu.VMEM)
ANY = pl.BlockSpec(memory_space=pl.ANY)


def room_for(*arrays):
    held = 0
    for a in arrays:
        rows, width = a.shape[-2], a.shape[-1]
        held += math.prod(a.shape[:-2]) * pl.cdiv(rows, 16 if rows % 8 else 8) * (
            16 if rows % 8 else 8
        ) * pl.cdiv(width, 128) * 128 * a.dtype.itemsize
    return held + 2 * 2**20
SMEM = pl.BlockSpec(memory_space=pltpu.SMEM)


def matmul(left, right):
    return jnp.dot(left, right, preferred_element_type=f32)


def contract_rows(left, right):
    return lax.dot_general(left, right, (((0,), (0,)), ((), ())), preferred_element_type=f32)


def times_transpose(left, right):
    return lax.dot_general(left, right, (((1,), (1,)), ((), ())), preferred_element_type=f32)


def layer_norm(values, gain):
    centered = values - jnp.mean(values, axis=-1, keepdims=True)
    variance = jnp.mean(centered * centered, axis=-1, keepdims=True)
    return centered * lax.rsqrt(variance + epsilon) * gain


def exact_gelu(values):
    return jax.nn.gelu(values, approximate=False)


def table_entry(table, index):
    places = jnp.arange(table.shape[0], dtype=jnp.int32)
    return jnp.sum(jnp.where(places == index, table, 0))


def swapped(value, axis, by=1):
    size = lax.axis_size(axis)
    return lax.ppermute(value, axis, [(i, i ^ by) for i in range(size)])


def position():
    return jnp.stack([lax.axis_index(a).astype(jnp.int32) for a in ALL])


def packed(shards, group):
    blocks, first = [], 0
    for i, shard in enumerate(shards):
        size = shard.shape[0] // group
        for column in range(0, shard.shape[1], D):
            blocks.append((i, column, first, size))
            first += size
    n_in = len(shards)

    def kernel(*refs):
        out, sems = refs[-2:]
        copies = [
            pltpu.make_async_copy(
                refs[i].at[:, :, pl.ds(column, D)], out.at[pl.ds(at, size)], sems.at[n]
            )
            for n, (i, column, at, size) in enumerate(blocks)
        ]
        for copy in copies:
            copy.start()
        for copy in copies:
            copy.wait()

    return pl.pallas_call(
        kernel,
        out_shape=jax.ShapeDtypeStruct((first, group, D), shards[0].dtype),
        in_specs=[pl.BlockSpec(memory_space=pltpu.HBM)] * n_in,
        out_specs=VMEM,
        scratch_shapes=[pltpu.SemaphoreType.DMA((len(blocks),))],
        compiler_params=pltpu.CompilerParams(vmem_limit_bytes=60 * 2**20),
        cost_estimate=NOTHING,
        name="packed",
    )(*(s.reshape(s.shape[0] // group, group, s.shape[1]) for s in shards))


def in_order(pieces, places, where, cut=None):
    n_in = len(pieces)
    count, groups = len(places), pieces[0].shape[1]
    spans = [(0, groups)] if cut is None else [(0, cut), (cut, groups - cut)]

    def kernel(at, *refs):
        first = 0
        for i in range(n_in):
            for j in range(pieces[i].shape[0]):
                z = jnp.bitwise_xor(at[0], places[first])
                for o, (start, size) in enumerate(spans):
                    refs[n_in + o][z] = refs[i][j, start : start + size]
                first += 1

    outs = pl.pallas_call(
        kernel,
        out_shape=[
            jax.ShapeDtypeStruct((count, size) + pieces[0].shape[2:], pieces[0].dtype)
            for _, size in spans
        ],
        in_specs=[SMEM] + [VMEM] * n_in,
        out_specs=[VMEM] * len(spans),
        compiler_params=pltpu.CompilerParams(vmem_limit_bytes=room_for(*pieces)),
        cost_estimate=NOTHING,
        name="in_order",
    )(where, *pieces)
    return outs[0] if cut is None else outs


def half_of(own, over_x, over_y, corners, where):
    count, groups, *tail = own.shape
    tail = tuple(tail)
    half = count // 2

    def kernel(at, own_ref, x_ref, y_ref, first_ref, second_ref, out_ref):
        y, x = at[1], at[3]
        out_ref[:, y, x] = own_ref[...]
        out_ref[:, y, 1 - x] = x_ref[...]
        out_ref[:, 1 - y, x] = y_ref[...]
        out_ref[:half, 1 - y, 1 - x] = first_ref[...]
        out_ref[half:, 1 - y, 1 - x] = second_ref[...]

    return pl.pallas_call(
        kernel,
        out_shape=jax.ShapeDtypeStruct((count, 2, 2, groups) + tail, own.dtype),
        in_specs=[SMEM] + [VMEM] * 5,
        out_specs=VMEM,
        compiler_params=pltpu.CompilerParams(vmem_limit_bytes=room_for(*[own] * 4)),
        cost_estimate=NOTHING,
        name="half_of",
    )(where, own, over_x, over_y, *corners)


def assembled(own, other, cuts, where):
    count, _, _, groups, group, width = own.shape
    step = count if count <= 8 else 1

    def kernel(at, *refs):
        for dc in range(2):
            c = jnp.bitwise_xor(at[2], dc)
            for o, (first, size, blocks) in enumerate(cuts):
                for b in range(blocks):
                    here = first + b * size
                    columns = slice(b * width, (b + 1) * width)
                    for z in range(step):
                        for y in range(2):
                            block = refs[dc][z, y, :, here : here + size]
                            refs[2 + o][z, y, c, :, :, :, columns] = block

    outs = [
        jax.ShapeDtypeStruct((count, 2, 2, 2, size, group, blocks * width), own.dtype)
        for _, size, blocks in cuts
    ]
    if step == count:
        specs = dict(in_specs=[SMEM, VMEM, VMEM], out_specs=[VMEM] * len(outs))
    else:
        specs = dict(
            grid=(count,),
            in_specs=[SMEM]
            + [pl.BlockSpec((1, 2, 2, groups, group, width), lambda z: (z, 0, 0, 0, 0, 0))] * 2,
            out_specs=[
                pl.BlockSpec((1,) + out.shape[1:], lambda z: (z, 0, 0, 0, 0, 0, 0)) for out in outs
            ],
        )
    return pl.pallas_call(
        kernel,
        out_shape=outs,
        compiler_params=pltpu.CompilerParams(
            vmem_limit_bytes=room_for(*outs) if step == count else 32 * 2**20
        ),
        cost_estimate=NOTHING,
        name="assembled",
        **specs,
    )(where, own, other)


def selection(where, core, slots, order):
    depth = 4 * len(order) * slots
    row = lax.broadcasted_iota(jnp.int32, (depth, 2 * depth), 0)
    column = lax.broadcasted_iota(jnp.int32, (depth, 2 * depth), 1)
    s, row = row % slots, row // slots
    z, row = jnp.zeros_like(row), row
    if len(order) > 1:
        step = row % len(order)
        bits, reversed_step = len(order).bit_length() - 1, jnp.zeros_like(row)
        for i in range(bits):
            reversed_step = reversed_step + ((step >> i) & 1) * (len(order) >> (i + 1))
        z = jnp.bitwise_xor(where[0], reversed_step)
        row = row // len(order)
    y, x = jnp.bitwise_xor(where[1], row // 2), jnp.bitwise_xor(where[3], row % 2)
    c = jnp.bitwise_xor(where[2], core)
    return (column == (((z * 2 + y) * 2 + c) * 2 + x) * slots + s).astype(bf16)


def mine_shapes(rows, width):
    return [jax.ShapeDtypeStruct((rows, width), f32)] + [
        jax.ShapeDtypeStruct((n, width), bf16) for n in (rows, rows, rows // 2, rows - rows // 2)
    ]


def taken_in(mine, received):
    _, rows, width = mine.shape
    half = rows // 2

    def kernel(mine_ref, got_ref, own, for_x, for_y, first, second):
        def total(side, at):
            return mine_ref[side, at].astype(f32) + got_ref[side, at].astype(f32)

        for i, ref in enumerate((own, for_x, for_y)):
            ref[...] = total(i, pl.ds(0, rows)).astype(ref.dtype)
        first[...] = total(3, pl.ds(0, half)).astype(bf16)
        second[...] = total(3, pl.ds(half, rows - half)).astype(bf16)

    out_shape = mine_shapes(rows, width)
    return pl.pallas_call(
        kernel,
        out_shape=out_shape,
        in_specs=[VMEM] * 2,
        out_specs=[VMEM] * 5,
        compiler_params=pltpu.CompilerParams(vmem_limit_bytes=room_for(*out_shape)),
        cost_estimate=NOTHING,
        name="taken_in",
    )(mine, received)


def sums_in_parts(where, arrays, products, memory_rows):
    order = z_places()
    slots = D // (8 * len(order))
    width = D * sum(arrays[right].shape[1] // D for _, right, _ in products if right is not None)
    width += sum(arrays[left].shape[0] for left, right, _ in products if right is None)
    given = []
    for core in range(2):
        pick = selection(where, core, slots, order)
        columns = []
        for left, right, first in products:
            turned = times_transpose(pick, arrays[left]).astype(bf16)
            if right is not None:
                turned = matmul(turned[:, first:], arrays[right]).astype(bf16)
            columns.append(turned)
        rows = jnp.concatenate(columns, axis=1).reshape(4, -1, width)
        if memory_rows:
            devices = []
            for side in range(4):
                y, x = jnp.bitwise_xor(where[1], side // 2), jnp.bitwise_xor(where[3], side % 2)
                c = jnp.bitwise_xor(where[2], core)
                devices += [((jnp.bitwise_xor(where[0], r) * 2 + y) * 2 + c) * 2 + x for r in order]
            key_grad, value_grad, key_weight, value_weight = arrays[-4:]
            grad = times_transpose(key_grad, key_weight) + times_transpose(value_grad, value_weight)
            whole = lax.dynamic_update_slice(
                jnp.zeros((8 * len(order) * memory_rows, D), bf16), grad.astype(bf16), (where[4], 0)
            )
            slabs = whole.reshape(8 * len(order), memory_rows, D)[jnp.stack(devices)]
            fold = width // D
            slabs = slabs.reshape(4, len(order), fold, memory_rows // fold, D)
            slabs = jnp.transpose(slabs, (0, 1, 3, 2, 4)).reshape(4, -1, width)
            rows = jnp.concatenate([rows, slabs], axis=1)
        given.append(rows)
    return given


def sums_out(where, arrays, products, memory_rows=0):
    order = z_places()
    slots = D // (8 * len(order))
    if slots % 8:
        return sums_in_parts(where, arrays, products, memory_rows)
    n_in = len(arrays)
    depth = slots * len(order)
    blocks, column = [], 0
    for left, right, first in products:
        wide = arrays[left].shape[0] if right is None else arrays[right].shape[1]
        for at in range(0, wide, D):
            size = min(D, wide - at)
            blocks.append((left, right, first, at, size, column))
            column += size
    width = column
    fold = width // D
    part = memory_rows // fold
    rows = depth + len(order) * part
    window = arrays[-4].shape[0] if memory_rows else 8

    def kernel(at, *refs):
        ins, outs, block_ref, grad_ref = refs[:n_in], refs[n_in : n_in + 2], refs[-2], refs[-1]

        def places(core):
            c = jnp.bitwise_xor(at[2], core)
            for side in range(4):
                y, x = jnp.bitwise_xor(at[1], side // 2), jnp.bitwise_xor(at[3], side % 2)
                for i, r in enumerate(order):
                    yield side, i, ((jnp.bitwise_xor(at[0], r) * 2 + y) * 2 + c) * 2 + x

        if memory_rows:
            key_grad, value_grad, key_weight, value_weight = ins[-4:]
            grad_ref[...] = times_transpose(key_grad[...], key_weight[...]) + times_transpose(
                value_grad[...], value_weight[...]
            )
            for core in (1, 0):
                for side, i, device in places(core):
                    start = device * memory_rows - at[4]
                    inside = (start >= 0) & (start + memory_rows <= window)
                    start = pl.multiple_of(jnp.where(inside, start, 0), memory_rows)
                    slab = grad_ref[pl.ds(start, memory_rows), :]
                    slab = jnp.where(inside, slab, jnp.zeros_like(slab)).astype(bf16)
                    for j in range(fold):
                        here = pl.ds(depth + i * part, part)
                        outs[core][side, here, j * D : (j + 1) * D] = slab[
                            j * part : (j + 1) * part
                        ]
        for n, (left, right, first, from_, size, to) in enumerate(blocks):
            if right is None:
                block = ins[left][...].astype(f32).T
            else:
                block = contract_rows(ins[left][first:, :], ins[right][:, from_ : from_ + size])
            slot = n % 2
            block_ref[slot, :, :, :size] = block.reshape(8 * len(order), slots, size)
            for core in (1, 0):
                for side, i, device in places(core):
                    slab = block_ref[slot, device, :, :size].astype(bf16)
                    outs[core][side, i * slots : (i + 1) * slots, to : to + size] = slab

    shape = jax.ShapeDtypeStruct((4, rows, width), bf16)
    return pl.pallas_call(
        kernel,
        out_shape=[shape, shape],
        in_specs=[SMEM] + [VMEM] * n_in,
        out_specs=[VMEM] * 2,
        scratch_shapes=[
            pltpu.VMEM((2, 8 * len(order), slots, D), f32),
            pltpu.VMEM((window, D), f32),
        ],
        compiler_params=pltpu.CompilerParams(
            vmem_limit_bytes=room_for(shape, shape) + 2 * D * D * 4 + window * D * 4 + 3 * 2**20
        ),
        cost_estimate=NOTHING,
        name="sums_out",
    )(where, *arrays)


def hidden_sums_out(where, activated, grad):
    hidden = activated.shape[1]
    order = z_places()
    span = hidden // len(order)
    slots = span // 8
    if span % 128 or slots % 8:
        given = []
        for core in range(2):
            pick = selection(where, core, slots, order)
            turned = times_transpose(pick, activated).astype(bf16)
            given.append(matmul(turned, grad).astype(bf16).reshape(4, -1, D))
        return given

    def kernel(at, act_ref, grad_ref, mine, other, block_ref):
        for i, r in enumerate(order):
            first = pl.multiple_of(jnp.bitwise_xor(at[0], r) * span, 128)
            block = contract_rows(act_ref[:, pl.ds(first, span)], grad_ref[...])
            block_ref[i % 2] = block.reshape(8, slots, D)
            for core, ref in ((1, other), (0, mine)):
                c = jnp.bitwise_xor(at[2], core)
                for side in range(4):
                    y, x = jnp.bitwise_xor(at[1], side // 2), jnp.bitwise_xor(at[3], side % 2)
                    slab = block_ref[i % 2, (y * 2 + c) * 2 + x].astype(bf16)
                    ref[side, i * slots : (i + 1) * slots, :] = slab

    shape = jax.ShapeDtypeStruct((4, len(order) * slots, D), bf16)
    return pl.pallas_call(
        kernel,
        out_shape=[shape, shape],
        in_specs=[SMEM] + [VMEM] * 2,
        out_specs=[VMEM] * 2,
        scratch_shapes=[pltpu.VMEM((2, 8, slots, D), f32)],
        compiler_params=pltpu.CompilerParams(
            vmem_limit_bytes=room_for(shape, shape) + 8 * 2**20
        ),
        cost_estimate=NOTHING,
        name="hidden_sums_out",
    )(where, activated, grad)


def hold(*values):
    return lax.optimization_barrier(values)


def z_first(shard):
    return swapped(shard[None], "z", lax.axis_size("z") // 2)


def z_rest(shard, received):
    by = lax.axis_size("z") // 2
    pieces, places = [shard[None], received], [0, by]
    while by > 1:
        by //= 2
        received = swapped(jnp.concatenate(pieces), "z", by)
        pieces, places = pieces + [received], places + [p ^ by for p in places]
    return pieces


def z_places():
    by, places = lax.axis_size("z") // 2, [0]
    while by:
        places = places + [p ^ by for p in places]
        by //= 2
    return places


def corners_in(over_x, over_y):
    half = over_x.shape[0] // 2
    return swapped(over_x[:half], "y"), swapped(over_y[half:], "x")


def corners_out(mine):
    return swapped(mine[3], "y"), swapped(mine[4], "x")


def sides_out(mine, corners):
    _, for_x, for_y = mine[:3]
    half = corners[0].shape[0]

    def kernel(x_ref, y_ref, first_ref, second_ref, x_out, y_out):
        x_out[:half] = (x_ref[:half].astype(f32) + first_ref[...].astype(f32)).astype(bf16)
        x_out[half:] = x_ref[half:]
        y_out[:half] = y_ref[:half]
        y_out[half:] = (y_ref[half:].astype(f32) + second_ref[...].astype(f32)).astype(bf16)

    shape = jax.ShapeDtypeStruct(for_x.shape, bf16)
    x_out, y_out = pl.pallas_call(
        kernel,
        out_shape=[shape, shape],
        in_specs=[VMEM] * 4,
        out_specs=[VMEM] * 2,
        compiler_params=pltpu.CompilerParams(vmem_limit_bytes=room_for(shape, shape)),
        cost_estimate=NOTHING,
        name="sides_out",
    )(for_x, for_y, *corners)
    return swapped(x_out, "x"), swapped(y_out, "y")


def halved(terms, parts):
    rows, width = terms[0].shape
    n_in = len(terms)

    def kernel(*refs):
        start, out = 0, 0
        for part in parts:
            half = part // 2
            for first, ref in ((start, refs[n_in]), (start + half, refs[n_in + 1])):
                total = sum(r[pl.ds(first, half), :].astype(f32) for r in refs[:n_in])
                ref[pl.ds(out, half), :] = total.astype(ref.dtype)
            start, out = start + part, out + half

    return pl.pallas_call(
        kernel,
        out_shape=[
            jax.ShapeDtypeStruct((rows // 2, width), f32),
            jax.ShapeDtypeStruct((rows // 2, width), bf16),
        ],
        in_specs=[VMEM] * n_in,
        out_specs=[VMEM] * 2,
        compiler_params=pltpu.CompilerParams(vmem_limit_bytes=room_for(terms[0])),
        cost_estimate=NOTHING,
        name="halved",
    )(*terms)


def z_most(terms, parts):
    by = 1
    keep, give = halved(terms, parts)
    received, parts = swapped(give, "z", by), [p // 2 for p in parts]
    while 2 * by < lax.axis_size("z") // 2:
        by *= 2
        keep, give = halved([keep, received], parts)
        received, parts = swapped(give, "z", by), [p // 2 for p in parts]
    return keep, received


def z_last(keep, received, parts):
    by = lax.axis_size("z") // 2
    keep, give = halved([keep, received], [p // by for p in parts])
    return keep, swapped(give, "z", by)


def plus(keep, received):
    return keep + received.astype(f32)


def lane_halves(block):
    lanes = lax.broadcasted_iota(jnp.int32, block.shape, 1)
    zero = jnp.zeros_like(block)
    return jnp.where(lanes < HEAD, block, zero), jnp.where(lanes < HEAD, zero, block)


def allowed_at(shape, first, bounds, causal):
    keys = first + lax.broadcasted_iota(jnp.int32, shape, 0)
    allowed = (keys >= bounds[0]) & (keys < bounds[1])
    if causal:
        queries = lax.broadcasted_iota(jnp.int32, shape, 1)
        allowed = allowed & (keys - shape[1] <= queries)
    return allowed


def key_block(width):
    return next(width // n for n in range(1, width) if width % (16 * n) == 0 and width // n <= 1536)


def attend_kernel(causal, block, bounds, q_ref, k_ref, v_ref, out_ref, low_ref, lse_ref):
    rows, width = q_ref.shape[0], k_ref.shape[0]

    def pair(h, carried):
        lanes = pl.ds(pl.multiple_of(h * PAIR, PAIR), PAIR)
        halves = lane_halves(q_ref[:, lanes] * SCALE)

        def step(i, state):
            first = pl.multiple_of(i * block, block)
            keys, values = k_ref[pl.ds(first, block), lanes], v_ref[pl.ds(first, block), lanes]
            allowed = allowed_at((block, rows), first, bounds, causal)
            new = []
            for half in range(2):
                peak, total, summed = state[half]
                scores = jnp.where(allowed, times_transpose(keys, halves[half]), big_negative)
                top = jnp.maximum(peak, jnp.max(scores, axis=0, keepdims=True))
                weights = jnp.exp(scores - top)
                factor = jnp.exp(peak - top)
                new.append(
                    (
                        top,
                        total * factor + jnp.sum(weights, axis=0, keepdims=True),
                        summed * factor + contract_rows(values, weights.astype(bf16)),
                    )
                )
            return tuple(new)

        start = (
            jnp.full((1, rows), big_negative, f32),
            jnp.zeros((1, rows), f32),
            jnp.zeros((PAIR, rows), f32),
        )
        state = (start, start)
        if width == block:
            state = step(0, state)
        else:
            state = lax.fori_loop(0, width // block, step, state)
        outs = [s[2] / s[1] for s in state]
        out = jnp.concatenate([outs[0][:HEAD], outs[1][HEAD:]], axis=0).T
        out_ref[:, lanes] = out
        low_ref[:, lanes] = out.astype(bf16)
        for half in range(2):
            lse_ref[h, half : half + 1, :] = state[half][0] + jnp.log(state[half][1])
        return carried

    lax.fori_loop(0, PAIRS, pair, 0)


def attend(queries, keys, values, bounds, causal):
    rows, width = queries.shape[0], keys.shape[0]
    block = key_block(width)
    out_shape = [
        jax.ShapeDtypeStruct((rows, D), f32),
        jax.ShapeDtypeStruct((rows, D), bf16),
        jax.ShapeDtypeStruct((PAIRS, 2, rows), f32),
    ]
    return pl.pallas_call(
        lambda *refs: attend_kernel(causal, block, *refs),
        in_specs=[SMEM] + [VMEM] * 3,
        out_specs=[VMEM] * 3,
        out_shape=out_shape,
        compiler_params=pltpu.CompilerParams(
            vmem_limit_bytes=6 * 2**20 if width <= 2048 else 40 * 2**20
        ),
        cost_estimate=NOTHING,
        name="attend_self" if causal else "attend_cross",
    )(bounds, queries, keys, values)


def attend_back_kernel(
    causal, block, bounds, q_ref, k_ref, v_ref, o_ref, g_ref, lse_ref, dq_ref, dk_ref, dv_ref
):
    rows, width = q_ref.shape[0], k_ref.shape[0]

    def pair(h, carried):
        lanes = pl.ds(pl.multiple_of(h * PAIR, PAIR), PAIR)
        query_halves = lane_halves(q_ref[:, lanes] * SCALE)
        grads = g_ref[:, lanes]
        grad_halves = lane_halves(grads)
        products = (grads.astype(f32) * o_ref[:, lanes]).T
        deltas = [
            jnp.sum(products[:HEAD], axis=0, keepdims=True),
            jnp.sum(products[HEAD:], axis=0, keepdims=True),
        ]

        def step(i, state):
            first = pl.multiple_of(i * block, block)
            keys, values = k_ref[pl.ds(first, block), lanes], v_ref[pl.ds(first, block), lanes]
            allowed = allowed_at((block, rows), first, bounds, causal)
            new, key_grad, value_grad = [], None, None
            for half in range(2):
                scores = jnp.where(allowed, times_transpose(keys, query_halves[half]), big_negative)
                probs = jnp.exp(scores - lse_ref[h, half : half + 1, :])
                value_part = matmul(probs.astype(bf16), grad_halves[half])
                slopes = times_transpose(values, grad_halves[half])
                score_grad = (probs * (slopes - deltas[half])).astype(bf16)
                key_part = matmul(score_grad, query_halves[half])
                new.append(state[half] + contract_rows(keys, score_grad))
                key_grad = key_part if key_grad is None else key_grad + key_part
                value_grad = value_part if value_grad is None else value_grad + value_part
            dk_ref[pl.ds(first, block), lanes] = key_grad.astype(bf16)
            dv_ref[pl.ds(first, block), lanes] = value_grad.astype(bf16)
            return tuple(new)

        zero = jnp.zeros((PAIR, rows), f32)
        state = (zero, zero)
        if width == block:
            state = step(0, state)
        else:
            state = lax.fori_loop(0, width // block, step, state)
        dq_ref[:, lanes] = (
            (jnp.concatenate([state[0][:HEAD], state[1][HEAD:]], axis=0) * SCALE)
            .T.astype(bf16)
        )
        return carried

    lax.fori_loop(0, PAIRS, pair, 0)


def attend_back(queries, keys, values, out, grad, lse, bounds, causal):
    rows, width = queries.shape[0], keys.shape[0]
    block = key_block(width)
    out_shape = [
        jax.ShapeDtypeStruct((rows, D), bf16),
        jax.ShapeDtypeStruct((width, D), bf16),
        jax.ShapeDtypeStruct((width, D), bf16),
    ]
    return pl.pallas_call(
        lambda *refs: attend_back_kernel(causal, block, *refs),
        in_specs=[SMEM] + [VMEM] * 6,
        out_specs=[VMEM] * 3,
        out_shape=out_shape,
        compiler_params=pltpu.CompilerParams(
            vmem_limit_bytes=11 * 2**20 if width <= 2048 else 60 * 2**20
        ),
        cost_estimate=NOTHING,
        name="attend_back_self" if causal else "attend_back_cross",
    )(bounds, queries, keys, values, out, grad, lse)


def activate(values, weight):
    rows, hidden = values.shape[0], weight.shape[1]
    step = min(hidden, D)

    def kernel(values_ref, weight_ref, out_ref, slope_ref):
        for at in range(0, hidden, step):
            inner = matmul(values_ref[...], weight_ref[:, at : at + step])
            below = 0.5 * (1.0 + lax.erf(inner * (0.5**0.5)))
            out_ref[:, at : at + step] = (inner * below).astype(bf16)
            bell = jnp.exp(-0.5 * inner * inner) * (1.0 / math.sqrt(2.0 * math.pi))
            slope_ref[:, at : at + step] = below + inner * bell

    return pl.pallas_call(
        kernel,
        out_shape=[
            jax.ShapeDtypeStruct((rows, hidden), bf16),
            jax.ShapeDtypeStruct((rows, hidden), f32),
        ],
        in_specs=[VMEM] * 2,
        out_specs=[VMEM] * 2,
        compiler_params=pltpu.CompilerParams(vmem_limit_bytes=8 * 2**20),
        cost_estimate=NOTHING,
        name="activate",
    )(values, weight)


def padded(shard, rows):
    return jnp.pad(shard, ((0, rows - shard.shape[0]), (0, 0)))


def grouped(shard, group):
    return shard.reshape(shard.shape[0] // group, group, shard.shape[1])


def per_device(
    tokens,
    memory,
    self_query,
    self_key,
    self_value,
    self_output,
    cross_query,
    cross_key,
    cross_value,
    cross_output,
    feed_in,
    feed_out,
    gain_self,
    gain_cross,
    gain_feed,
    doc_lengths,
    seg_doc,
    cotangent,
):
    where = position()
    token_rows = tokens.shape[0]
    count = lax.axis_size("z") * 8
    slots = self_query.shape[0]
    memory_rows = memory.shape[0]
    group = math.gcd(8, slots) if slots % 4 == 0 else slots
    memory_groups = pl.cdiv(memory_rows, group)
    gain_groups = pl.cdiv(3, group)
    gain_rows = gain_groups * group
    slot_groups = slots // group

    gains = jnp.pad(jnp.stack([gain_self, gain_cross, gain_feed]), ((0, gain_rows - 3), (0, D - slots)))
    hidden = feed_in.shape[1]
    places = z_places()
    cuts1 = [(i * slot_groups, slot_groups, 1) for i in range(4)]
    cuts1.append((4 * slot_groups, gain_groups, 1))
    cuts2 = [(i * slot_groups, slot_groups, 1) for i in range(3)]
    cuts2.append((3 * slot_groups, memory_groups, 1))
    cuts3 = [(0, slot_groups, 1), (slot_groups, slot_groups, hidden // D)]
    cuts4 = [(0, feed_out.shape[0] // group, 1)]
    s1 = packed([self_query, self_key, self_value, self_output, gains], group)
    s2 = packed(
        [cross_query, cross_key, cross_value, padded(memory, memory_groups * group)], group
    )
    s3 = packed([cross_output, feed_in], group)
    s4 = grouped(feed_out, group)

    a1 = z_first(s1)
    earlier = lax.ppermute(tokens, "x", [(0, 1)])
    a1, s2, s3, s4 = hold(a1, s2, s3, s4)
    b1 = z_rest(s1, a1)
    a2 = z_first(s2)
    own1 = in_order(b1, places, where)
    own1, a2, earlier, s3, s4, doc_lengths, seg_doc = hold(
        own1, a2, earlier, s3, s4, doc_lengths, seg_doc
    )
    x1, y1 = swapped(own1, "x"), swapped(own1, "y")
    b2 = z_rest(s2, a2)
    a3 = z_first(s3)
    window = count * memory_rows // 2 + memory_rows
    ends = jnp.cumsum(doc_lengths)
    document = table_entry(seg_doc, (where[0] * 2 + where[1]) * 2 + where[2])
    doc_end = table_entry(ends, document)
    doc_start = doc_end - table_entry(doc_lengths, document)
    window_start = jnp.minimum(
        doc_start // memory_rows * memory_rows, count * memory_rows - window
    ).astype(jnp.int32)
    cross_bounds = jnp.stack([doc_start - window_start, doc_end - window_start]).astype(jnp.int32)
    where_window = jnp.concatenate([where, window_start[None]])
    self_bounds = jnp.stack(
        [jnp.where(where[3] == 0, token_rows, 0), jnp.int32(2 * token_rows)]
    ).astype(jnp.int32)
    both_tokens = jnp.concatenate([earlier, tokens], axis=0)
    own2 = in_order(b2, places, where)
    own2, x1, y1, own1, both_tokens, where_window, cross_bounds, self_bounds, s4 = hold(
        own2, x1, y1, own1, both_tokens, where_window, cross_bounds, self_bounds, s4
    )

    d1 = corners_in(x1, y1)
    x2, y2 = swapped(own2, "x"), swapped(own2, "y")
    b3 = z_rest(s3, a3)
    own3 = in_order(b3, places, where)
    a4 = z_first(s4)
    d1, x2, y2, own2, own3, a4 = hold(d1, x2, y2, own2, own3, a4)

    d2 = corners_in(x2, y2)
    x3, y3 = swapped(own3, "x"), swapped(own3, "y")
    half1 = half_of(own1, x1, y1, d1, where)
    c1 = swapped(half1, "c")
    wholes = assembled(half1, c1, cuts1, where)
    self_query, self_key, self_value, self_output = (w.reshape(D, D) for w in wholes[:4])
    a4, s4, self_query = hold(a4, s4, self_query)
    b4 = z_rest(s4, a4)
    own4 = in_order(b4, places, where)
    gains = wholes[4].reshape(count, gain_rows, D)[:, :3, :slots]
    gain_self, gain_cross, gain_feed = (
        gains[:, i].reshape(D).astype(f32) for i in range(3)
    )
    queries = matmul(tokens, self_query).astype(bf16)
    keys = matmul(both_tokens, self_key).astype(bf16)
    values = matmul(both_tokens, self_value).astype(bf16)
    self_full, self_out, self_lse = attend(queries, keys, values, self_bounds, True)
    mid_self = tokens.astype(f32) + matmul(self_out, self_output)
    hidden_self, back_self = jax.vjp(layer_norm, mid_self, gain_self)
    hidden_self_low = hidden_self.astype(bf16)
    d2, x3, y3, own3, own4, hidden_self, hidden_self_low = hold(
        d2, x3, y3, own3, own4, hidden_self, hidden_self_low
    )

    d3 = corners_in(x3, y3)
    x4, y4 = swapped(own4, "x"), swapped(own4, "y")
    half2 = half_of(own2, x2, y2, d2, where)
    c2 = swapped(half2, "c")
    wholes = assembled(half2, c2, cuts2, where)
    cross_query, cross_key, cross_value = (w.reshape(D, D) for w in wholes[:3])
    memory_all = wholes[3].reshape(count, memory_groups * group, D)[:, :memory_rows]
    memory_all = memory_all.reshape(count * memory_rows, D)
    memory_here = lax.dynamic_slice(memory_all, (where_window[4], 0), (window, D))
    cross_queries = matmul(hidden_self_low, cross_query).astype(bf16)
    memory_keys = matmul(memory_here, cross_key).astype(bf16)
    memory_values = matmul(memory_here, cross_value).astype(bf16)
    cross_full, cross_out, cross_lse = attend(
        cross_queries, memory_keys, memory_values, cross_bounds, False
    )
    d3, x4, y4, own4, cross_out = hold(d3, x4, y4, own4, cross_out)

    d4 = corners_in(x4, y4)
    half3 = half_of(own3, x3, y3, d3, where)
    c3 = swapped(half3, "c")
    wholes = assembled(half3, c3, cuts3, where)
    cross_output, feed_in = (w.reshape(D, w.shape[-1]) for w in wholes)
    mid_cross = hidden_self + matmul(cross_out, cross_output)
    hidden_cross, back_cross = jax.vjp(layer_norm, mid_cross, gain_cross)
    hidden_cross_low = hidden_cross.astype(bf16)
    activated, slope = activate(hidden_cross_low, feed_in)
    d4, activated, own4 = hold(d4, activated, own4)
    half4 = half_of(own4, x4, y4, d4, where)
    c4 = swapped(half4, "c")
    wholes = assembled(half4, c4, cuts4, where)
    feed_out = wholes[0].reshape(hidden, D)
    mid_feed = hidden_cross + matmul(activated, feed_out)
    layer_out, back_feed = jax.vjp(layer_norm, mid_feed, gain_feed)
    gradient_feed_mid, gain_feed_sum = back_feed(cotangent.astype(f32))
    feed_rounded = gradient_feed_mid.astype(bf16)
    m4, o4 = hidden_sums_out(where, activated, feed_rounded)
    m4, o4, feed_rounded = hold(m4, o4, feed_rounded)
    r4 = swapped(o4, "c")
    gradient_inner = (times_transpose(feed_rounded, feed_out) * slope).astype(bf16)
    m3, o3 = sums_out(where, [hidden_cross_low, gradient_inner], [(0, 1, 0)])
    r4, m3, o3, gradient_inner = hold(r4, m3, o3, gradient_inner)
    m4 = taken_in(m4, r4)
    d4 = corners_out(m4)
    r3 = swapped(o3, "c")
    gradient_hidden_cross = gradient_feed_mid + times_transpose(gradient_inner, feed_in)
    gradient_cross_mid, gain_cross_sum = back_cross(gradient_hidden_cross)
    cross_rounded = gradient_cross_mid.astype(bf16)

    outgoing = times_transpose(cross_rounded, cross_output).astype(bf16)
    r3, d4, outgoing, cross_rounded = hold(r3, d4, outgoing, cross_rounded)
    x4, y4 = sides_out(m4, d4)
    m3 = taken_in(m3, r3)
    d3 = corners_out(m3)
    cross_query_grad, memory_key_grad, memory_value_grad = attend_back(
        cross_queries,
        memory_keys,
        memory_values,
        cross_full,
        outgoing,
        cross_lse,
        cross_bounds,
        False,
    )
    x4, y4, d3, cross_query_grad, memory_key_grad, memory_value_grad, cross_rounded = hold(
        x4, y4, d3, cross_query_grad, memory_key_grad, memory_value_grad, cross_rounded
    )
    x3, y3 = sides_out(m3, d3)
    parts4, parts2, parts1 = [hidden // 8], [D // 8, count * memory_rows // 32], [D // 8]
    k4 = z_most([m4[0], x4, y4], parts4)
    m2, o2 = sums_out(
        where_window,
        [
            hidden_self_low,
            cross_query_grad,
            memory_here,
            cross_out,
            cross_rounded,
            memory_key_grad,
            memory_value_grad,
            cross_key,
            cross_value,
        ],
        [(0, 1, 0), (2, 5, 0), (2, 6, 0), (3, 4, 0)],
        memory_rows,
    )
    x3, y3, k4, m2, o2, cross_query_grad = hold(x3, y3, k4, m2, o2, cross_query_grad)
    r2 = swapped(o2, "c")
    k3 = z_most([m3[0], x3, y3], parts1)
    k4 = z_last(*k4, parts4)
    gradient_hidden_self = gradient_cross_mid + times_transpose(cross_query_grad, cross_query)
    gradient_self_mid, gain_self_sum = back_self(gradient_hidden_self)
    self_rounded = gradient_self_mid.astype(bf16)
    self_outgoing = times_transpose(self_rounded, self_output).astype(bf16)

    query_grad, key_grad, value_grad = attend_back(
        queries, keys, values, self_full, self_outgoing, self_lse, self_bounds, True
    )
    r2, k3, k4, query_grad, key_grad, value_grad, self_rounded = hold(
        r2, k3, k4, query_grad, key_grad, value_grad, self_rounded
    )
    m2 = taken_in(m2, r2)
    d2 = corners_out(m2)
    k3 = z_last(*k3, parts1)
    gain_sums = jnp.pad(
        jnp.stack([gain_self_sum, gain_cross_sum, gain_feed_sum]).astype(bf16),
        ((0, 128 - 3), (0, 0)),
    )
    m1, o1 = sums_out(
        where,
        [
            both_tokens,
            query_grad,
            key_grad,
            value_grad,
            self_out,
            self_rounded,
            gain_sums,
        ],
        [(0, 1, token_rows), (0, 2, 0), (0, 3, 0), (4, 5, 0), (6, None, 0)],
    )
    m1, o1, query_grad, key_grad, value_grad = hold(m1, o1, query_grad, key_grad, value_grad)
    r1 = swapped(o1, "c")
    both_grad = times_transpose(key_grad, self_key) + times_transpose(value_grad, self_value)
    d2, k3, r1, both_grad = hold(d2, k3, r1, both_grad)
    x2, y2 = sides_out(m2, d2)
    sent_back = lax.ppermute(both_grad[:token_rows].astype(bf16), "x", [(1, 0)])
    m1 = taken_in(m1, r1)
    d1 = corners_out(m1)
    partial_tokens = (
        gradient_self_mid + times_transpose(query_grad, self_query) + both_grad[token_rows:]
    )
    x2, y2, d1, partial_tokens = hold(x2, y2, d1, partial_tokens)
    x1, y1 = sides_out(m1, d1)
    k2 = z_most([m2[0], x2, y2], parts2)
    total_feed_out = plus(*k4)
    total_feed_in = plus(*k3)
    k2 = z_last(*k2, parts2)
    k2, x1, y1, total_feed_in, total_feed_out = hold(k2, x1, y1, total_feed_in, total_feed_out)
    k1 = z_most([m1[0], x1, y1], parts1)
    k1 = z_last(*k1, parts1)
    total_cross = plus(*k2)
    gradient_tokens = plus(partial_tokens, sent_back)
    total_self = plus(*k1)

    self_parts = [total_self[:, i * D : (i + 1) * D] for i in range(4)]
    cross_parts = [total_cross[:slots, i * D : (i + 1) * D] for i in range(4)]
    return (
        layer_out.astype(bf16),
        gradient_tokens,
        jnp.concatenate([total_cross[slots:, i * D : (i + 1) * D] for i in range(4)]),
        *self_parts,
        *cross_parts,
        total_feed_in,
        total_feed_out,
        total_self[:, 4 * D],
        total_self[:, 4 * D + 1],
        total_self[:, 4 * D + 2],
    )


def solution(mesh):
    fine = Mesh(mesh.devices.reshape(-1, 2, 2, 2), ALL)
    rows = P(ALL, None)
    return jax.shard_map(
        per_device,
        mesh=fine,
        in_specs=(rows,) * 12 + (P(ALL),) * 3 + (P(), P(), rows),
        out_specs=(rows,) * 13 + (P(ALL),) * 3,
        check_vma=False,
    )
```

time: 466 us -> 326 us (0.70)
  waiting for transfers between devices: 165 us -> 114 us
  matrix products: 65.7 us -> 15 us
  Pallas kernels: 94.7 us -> 81.3 us
  local copies, waits for them, and re-layouts: 32.6 us -> 20.1 us
  other arithmetic: 26.8 us -> 17.8 us
    ppermute x60 -> x56, waiting for transfers between devices: 165 us -> 114 us  [swapped(): return lax.ppermute(value, axis, [(i, i ^ by) for i in range(size)])]
    dot_general x10 -> x0, matrix products: 24 us -> none  [contract_rows(): lax.dot_general(left, right, (((0,), (0,)), ((), ())), preferred_element_...]
    dot_general x10 -> x9, matrix products: 24.8 us -> 8 us  [matmul(): return jnp.dot(left, right, preferred_element_type=f32)]
    pallas_call x16 -> x40, Pallas kernels: 94.7 us -> 81.3 us  [the longest x2 21 us: attend_back(): pl.pallas_call(lambda *refs: attend_back_kernel(causal, block, *refs), in...]
    dot_general x10 -> x8, matrix products: 16.9 us -> 7.03 us  [times_transpose(): lax.dot_general(left, right, (((1,), (1,)), ((), ())), preferred_element_...]
    dynamic_update_slice x1 -> x0, local copies, waits for them, and re-layouts: 8.38 us -> none  [per_device(): lax.dynamic_update_slice(jnp.zeros((2 * window, D), bf16), (times_transpo...]
    slice x0 -> x13, local copies, waits for them, and re-layouts: none -> 8.36 us  [the longest x8 5.6 us: corners_in(): return (swapped(over_x[:half], 'y'), swapped(over_y[half:], 'x'))]
    convert_element_type x8 -> x5, other arithmetic: 11.2 us -> 2.98 us  [the longest x1 2.47 us: per_device(): hidden_self_low = hidden_self.astype(bf16)]
  transfers between devices with their start and end apart: 62 -> 58, of which waited for: 23 -> 25; matrix products, arithmetic and copies ran while one was open for 16% -> 11% of each run, Pallas kernels for 12% -> 21%
where the time goes in v2:
time: 326 us; the launch traced here: 321 us
  waiting for transfers between devices  114 us (35%)
  Pallas kernels  81.3 us (25%)
  starting transfers between devices  66.4 us (20%)
  local copies, waits for them, and re-layouts  20.1 us (6%)
  other arithmetic  17.8 us (5%)
  matrix products  15 us (5%)
  between operations  6.35 us (2%)
    ppermute x56, waiting for transfers between devices, swapped(): return lax.ppermute(value, axis, [(i, i ^ by) for i in range(size)])  114 us
    ppermute x56, starting transfers between devices, swapped(): return lax.ppermute(value, axis, [(i, i ^ by) for i in range(size)])  61.7 us
    pallas_call x2, Pallas kernels, attend_back(): pl.pallas_call(lambda *refs: attend_back_kernel(causal, block, *refs), in...  21 us
    pallas_call x2, Pallas kernels, attend(): pl.pallas_call(lambda *refs: attend_kernel(causal, block, *refs), in_spec...  18.8 us
    pallas_call x3, Pallas kernels, sums_out(): pl.pallas_call(kernel, out_shape=[shape, shape], in_specs=[SMEM] + [VMEM]...  14 us
    unnamed x164, local copies, waits for them, and re-layouts  10.9 us
    dot_general x9, matrix products, matmul(): return jnp.dot(left, right, preferred_element_type=f32)  8 us
    pallas_call x4, Pallas kernels, assembled(): pl.pallas_call(kernel, out_shape=outs, compiler_params=pltpu.CompilerPara...  7.47 us
  transfers between devices with their start and end apart: 58, of which 25 were waited for; matrix products, arithmetic and copies ran while one was open for 11% of the time, Pallas kernels for 21%

profile of v2, /device:TPU:0, one launch (start us, length us, event | category | flops | bytes accessed | tf_op | source)
XLA Modules:
  0.0 321.5 jit_solution(10246577380198237420)
XLA Ops:
  3.5 4.1 %collective-permute-start = (bf16[1,13,8,768]{3,2,1,0:T(8,128)(2,1)}, bf16[1,13,8,768]{3,2,1,0:T(8,128)(2,1)S(1)}, u32[]{:S(2)}, u32[]{:S(2)}) collective-permute-start(bf16[1,13,8,768]{3,2,1,0:T(8,128)(2,1)} %bitcast.107), channel_id=1, source_target_pairs={{0,16},{8,24},{16,0},{24,8},{1,17},{9,25},{17,1},{25,9},{2,18},{10... | collective-permute-start | bytes 479240 | tf_op jit(solution)/shard_map/ppermute | solution.py:68
  7.6 3.4 %collective-permute-start.3 = (bf16[256,768]{1,0:T(8,128)(2,1)}, bf16[256,768]{1,0:T(8,128)(2,1)S(1)}, u32[]{:S(2)}, u32[]{:S(2)}) collective-permute-start(bf16[256,768]{1,0:T(8,128)(2,1)} %param.18), channel_id=1, source_target_pairs={{0,1},{2,3},{4,5},{6,7},{8,9},{10,11},{12,13},{14,15},{16,17},{18,... | collective-permute-start | bytes 1179656 | tf_op jit(solution)/shard_map/ppermute | solution.py:753
  17.2 3.3 %collective-permute-start.2 = (bf16[1,17,8,768]{3,2,1,0:T(8,128)(2,1)}, bf16[1,17,8,768]{3,2,1,0:T(8,128)(2,1)S(1)}, u32[]{:S(2)}, u32[]{:S(2)}) collective-permute-start(bf16[1,17,8,768]{3,2,1,0:T(8,128)(2,1)} %bitcast.101), channel_id=1, source_target_pairs={{0,16},{8,24},{16,0},{24,8},{1,17},{9,25},{17,1},{25,9},{2,18},{10... | collective-permute-start | bytes 626696 | tf_op jit(solution)/shard_map/ppermute | solution.py:68
  20.5 9.0 %collective-permute-done.1.refs_2_ = bf16[2,13,8,768]{3,2,1,0:T(8,128)(2,1)S(1)} collective-permute-done((bf16[2,13,8,768]{3,2,1,0:T(8,128)(2,1)S(1)}, bf16[2,13,8,768]{3,2,1,0:T(8,128)(2,1)S(1)}, u32[]{:S(2)}, u32[]{:S(2)}) %collective-permute-start.1) | collective-permute-done | bytes 319520 | tf_op jit(solution)/shard_map/ppermute | solution.py:68
  34.1 2.6 collective-permute-start.4
  43.1 2.5 collective-permute-done.4.refs_2_
  47.8 3.6 %collective-permute-start.11 = (bf16[1,15,8,768]{3,2,1,0:T(8,128)(2,1)S(1)}, bf16[1,15,8,768]{3,2,1,0:T(8,128)(2,1)S(1)}, u32[]{:S(2)}, u32[]{:S(2)}) collective-permute-start(bf16[1,15,8,768]{3,2,1,0:T(8,128)(2,1)S(1)} %bitcast.104), channel_id=1, source_target_pairs={{0,16},{8,24},{16,0},{24,8},{1,17},{9,25},{17,1},{25,9},{2,18},{10... | collective-permute-start | bytes 552968 | tf_op jit(solution)/shard_map/ppermute | solution.py:68
  51.3 7.1 %collective-permute-done.11.refs_1_ = bf16[1,15,8,768]{3,2,1,0:T(8,128)(2,1)S(1)} collective-permute-done((bf16[1,15,8,768]{3,2,1,0:T(8,128)(2,1)S(1)}, bf16[1,15,8,768]{3,2,1,0:T(8,128)(2,1)S(1)}, u32[]{:S(2)}, u32[]{:S(2)}) %collective-permute-start.11) | collective-permute-done | bytes 184352 | tf_op jit(solution)/shard_map/ppermute | solution.py:68
  60.7 5.3 %collective-permute-done.12.refs_2_ = bf16[2,15,8,768]{3,2,1,0:T(8,128)(2,1)S(1)} collective-permute-done((bf16[2,15,8,768]{3,2,1,0:T(8,128)(2,1)S(1)}, bf16[2,15,8,768]{3,2,1,0:T(8,128)(2,1)S(1)}, u32[]{:S(2)}, u32[]{:S(2)}) %collective-permute-start.12) | collective-permute-done | bytes 368672 | tf_op jit(solution)/shard_map/ppermute | solution.py:68
  66.0 2.8 collective-permute-start.13
  69.5 4.3 %collective-permute-done.13.refs_1_ = bf16[1,12,8,768]{3,2,1,0:T(8,128)(2,1)S(1)} collective-permute-done((bf16[1,12,8,768]{3,2,1,0:T(8,128)(2,1)S(1)}, bf16[1,12,8,768]{3,2,1,0:T(8,128)(2,1)S(1)}, u32[]{:S(2)}, u32[]{:S(2)}) %collective-permute-start.13) | collective-permute-done | bytes 147488 | tf_op jit(solution)/shard_map/ppermute | solution.py:68
  84.1 7.1 %attend_self.1 = (f32[256,768]{1,0:T(8,128)S(1)}, bf16[256,768]{1,0:T(8,128)(2,1)S(1)}, f32[6,2,256]{2,1,0:T(2,128)S(1)}) custom-call(s32[2]{0:T(128)S(1)} %get-tuple-element.224.refs_0_, bf16[256,768]{1,0:T(8,128)(2,1)S(1)} %fusion.1.refs_1_, bf16[512,768]{1,0:T(8,128)(2,1)S(1)} %convolution_convert_fusion.3.refs_2_, ...), custom_call_target="tpu_custom_call" | custom-call | flops 1 | bytes 1 | tf_op jit(solution)/shard_map/attend_self/pallas_call | solution.py:587
  94.3 2.7 collective-permute-start.19
  97.4 2.5 fusion.31
  99.9 3.9 %collective-permute-done.19.refs_2_ = bf16[2,12,8,768]{3,2,1,0:T(8,128)(2,1)S(1)} collective-permute-done((bf16[2,12,8,768]{3,2,1,0:T(8,128)(2,1)}, bf16[2,12,8,768]{3,2,1,0:T(8,128)(2,1)S(1)}, u32[]{:S(2)}, u32[]{:S(2)}) %collective-permute-start.19) | collective-permute-done | bytes 294944 | tf_op jit(solution)/shard_map/ppermute | solution.py:68
  124.1 11.7 %attend_cross.1 = (f32[256,768]{1,0:T(8,128)S(1)}, bf16[256,768]{1,0:T(8,128)(2,1)S(1)}, f32[6,2,256]{2,1,0:T(2,128)S(1)}) custom-call(s32[2]{0:T(128)S(1)} %get-tuple-element.236.refs_0_, bf16[256,768]{1,0:T(8,128)(2,1)S(1)} %convolution_convert_fusion.7.refs_1_, bf16[1088,768]{1,0:T(8,128)(2,1)S(1)} %convolution_convert_fusion.1.refs_2_, ...), custom_call_target="tpu_custom_call" | custom-call | flops 1 | bytes 1 | tf_op jit(solution)/shard_map/attend_cross/pallas_call | solution.py:587
  152.2 4.4 %collective-permute-done.28.refs_1_ = bf16[4,2,2,12,8,768]{5,4,3,2,1,0:T(8,128)(2,1)} collective-permute-done((bf16[4,2,2,12,8,768]{5,4,3,2,1,0:T(8,128)(2,1)S(1)}, bf16[4,2,2,12,8,768]{5,4,3,2,1,0:T(8,128)(2,1)}, u32[]{:S(2)}, u32[]{:S(2)}) %collective-permute-start.28) | collective-permute-done | bytes 2359328 | tf_op jit(solution)/shard_map/ppermute | solution.py:68
  162.0 2.5 hidden_sums_out.1
  166.2 2.5 sums_out.3
  174.6 4.7 %collective-permute-done.31.first_ref = bf16[192,768]{1,0:T(8,128)(2,1)S(1)} collective-permute-done((bf16[192,768]{1,0:T(8,128)(2,1)S(1)}, bf16[192,768]{1,0:T(8,128)(2,1)S(1)}, u32[]{:S(2)}, u32[]{:S(2)}) %collective-permute-start.31) | collective-permute-done | bytes 294944 | tf_op jit(solution)/shard_map/ppermute | solution.py:68
  184.5 13.3 %attend_back_cross.1 = (bf16[256,768]{1,0:T(8,128)(2,1)S(1)}, bf16[1088,768]{1,0:T(8,128)(2,1)S(1)}, bf16[1088,768]{1,0:T(8,128)(2,1)S(1)}) custom-call(s32[2]{0:T(128)S(1)} %get-tuple-element.236.refs_0_, bf16[256,768]{1,0:T(8,128)(2,1)S(1)} %copy-done.17, bf16[1088,768]{1,0:T(8,128)(2,1)S(1)} %copy-done.5, bf16[1088,768]{1,0:T(8,128)(2,1)S(1)} %copy-done.3, ...), custom_call_target="tpu_custom_call" | custom-call | flops 1 | bytes 1 | tf_op jit(solution)/shard_map/attend_back_cross/pallas_call | solution.py:658
  197.8 3.2 collective-permute-done.35.first_ref
  206.2 8.3 %sums_out.4 = (bf16[4,160,3072]{2,1,0:T(8,128)(2,1)S(1)}, bf16[4,160,3072]{2,1,0:T(8,128)(2,1)S(1)}) custom-call(s32[5]{0:T(128)S(1)} %concatenate.25.at, bf16[256,768]{1,0:T(8,128)(2,1)S(1)} %copy-done.15, bf16[256,768]{1,0:T(8,128)(2,1)S(1)} %get-tuple-element.320.refs_1_, bf16[1088,768]{1,0:T(8,128)(2,1)S(1)} %copy-done.1, ...), custom_call_target="tpu_custom_call" | custom-call | flops 1 | bytes 1 | tf_op jit(solution)/shard_map/sums_out/pallas_call | solution.py:349
  222.7 7.7 %attend_back_self.1 = (bf16[256,768]{1,0:T(8,128)(2,1)S(1)}, bf16[512,768]{1,0:T(8,128)(2,1)S(1)}, bf16[512,768]{1,0:T(8,128)(2,1)S(1)}) custom-call(s32[2]{0:T(128)S(1)} %get-tuple-element.224.refs_0_, bf16[256,768]{1,0:T(8,128)(2,1)S(1)} %copy-done.19, bf16[512,768]{1,0:T(8,128)(2,1)S(1)} %copy-done.25, bf16[512,768]{1,0:T(8,128)(2,1)S(1)} %copy-done.23, ...), custom_call_target="tpu_custom_call" | custom-call | flops 1 | bytes 1 | tf_op jit(solution)/shard_map/attend_back_self/pallas_call | solution.py:658
  230.5 3.2 sums_out.5
  239.5 8.0 %collective-permute-done.45 = bf16[24,3072]{1,0:T(8,128)(2,1)S(1)} collective-permute-done((bf16[24,3072]{1,0:T(8,128)(2,1)S(1)}, bf16[24,3072]{1,0:T(8,128)(2,1)S(1)}, u32[]{:S(2)}, u32[]{:S(2)}) %collective-permute-start.45) | collective-permute-done | bytes 147488 | tf_op jit(solution)/shard_map/ppermute | solution.py:68
  257.0 23.2 %collective-permute-done.49.first_ref = bf16[48,3200]{1,0:T(8,128)(2,1)S(1)} collective-permute-done((bf16[48,3200]{1,0:T(8,128)(2,1)S(1)}, bf16[48,3200]{1,0:T(8,128)(2,1)S(1)}, u32[]{:S(2)}, u32[]{:S(2)}) %collective-permute-start.49) | collective-permute-done | bytes 307232 | tf_op jit(solution)/shard_map/ppermute | solution.py:68
  283.5 9.7 %collective-permute-done.52.refs_1_ = bf16[80,3072]{1,0:T(8,128)(2,1)S(1)} collective-permute-done((bf16[80,3072]{1,0:T(8,128)(2,1)S(1)}, bf16[80,3072]{1,0:T(8,128)(2,1)S(1)}, u32[]{:S(2)}, u32[]{:S(2)}) %collective-permute-start.52) | collective-permute-done | bytes 491552 | tf_op jit(solution)/shard_map/ppermute | solution.py:68
  295.9 5.1 %collective-permute-done.54.refs_1_ = bf16[96,3200]{1,0:T(8,128)(2,1)S(1)} collective-permute-done((bf16[96,3200]{1,0:T(8,128)(2,1)S(1)}, bf16[96,3200]{1,0:T(8,128)(2,1)S(1)}, u32[]{:S(2)}, u32[]{:S(2)}) %collective-permute-start.54) | collective-permute-done | bytes 614432 | tf_op jit(solution)/shard_map/ppermute | solution.py:68
  300.9 3.1 collective-permute-done.53
  305.1 6.9 %collective-permute-done.56.refs_1_ = bf16[48,3200]{1,0:T(8,128)(2,1)S(1)} collective-permute-done((bf16[48,3200]{1,0:T(8,128)(2,1)S(1)}, bf16[48,3200]{1,0:T(8,128)(2,1)S(1)}, u32[]{:S(2)}, u32[]{:S(2)}) %collective-permute-start.56) | collective-permute-done | bytes 307232 | tf_op jit(solution)/shard_map/ppermute | solution.py:68
  313.6 6.2 %collective-permute-done.57 = bf16[24,3200]{1,0:T(8,128)(2,1)S(1)} collective-permute-done((bf16[24,3200]{1,0:T(8,128)(2,1)S(1)}, bf16[24,3200]{1,0:T(8,128)(2,1)S(1)}, u32[]{:S(2)}, u32[]{:S(2)}) %collective-permute-start.57) | collective-permute-done | bytes 153632 | tf_op jit(solution)/shard_map/ppermute | solution.py:68
  (376 shorter events, 127.3 us)
Async XLA Ops:
  7.6 22.6 %collective-permute-start.3 = (bf16[256,768]{1,0:T(8,128)(2,1)}, bf16[256,768]{1,0:T(8,128)(2,1)S(1)}, u32[]{:S(2)}, u32[]{:S(2)}) collective-permute-start(bf16[256,768]{1,0:T(8,128)(2,1)} %param.18), channel_id=1, source_target_pairs={{0,1},{2,3},{4,5},{6,7},{8,9},{10,11},{12,13},{14,15},{16,17},{18,... | collective-permute-start | bytes 1179656 | tf_op jit(solution)/shard_map/ppermute | solution.py:753
  30.2 16.0 %collective-permute-start.5 = (bf16[4,13,8,768]{3,2,1,0:T(8,128)(2,1)S(1)}, bf16[4,13,8,768]{3,2,1,0:T(8,128)(2,1)S(1)}, u32[]{:S(2)}, u32[]{:S(2)}) collective-permute-start(bf16[4,13,8,768]{3,2,1,0:T(8,128)(2,1)S(1)} %in_order.4.own_ref), channel_id=1, source_target_pairs={{0,1},{1,0},{2,3},{3,2},{4,5},{5,4},{6,7},{7,6},{8,9},{9,8},{10,11... | collective-permute-start | bytes 1916936 | tf_op jit(solution)/shard_map/ppermute | solution.py:68
  31.6 14.7 %collective-permute-start.6 = (bf16[4,13,8,768]{3,2,1,0:T(8,128)(2,1)S(1)}, bf16[4,13,8,768]{3,2,1,0:T(8,128)(2,1)S(1)}, u32[]{:S(2)}, u32[]{:S(2)}) collective-permute-start(bf16[4,13,8,768]{3,2,1,0:T(8,128)(2,1)S(1)} %in_order.4.own_ref), channel_id=1, source_target_pairs={{0,4},{4,0},{1,5},{5,1},{2,6},{6,2},{3,7},{7,3},{8,12},{12,8},{9,1... | collective-permute-start | bytes 1916936 | tf_op jit(solution)/shard_map/ppermute | solution.py:68
  46.2 27.6 %collective-permute-start.10 = (bf16[4,17,8,768]{3,2,1,0:T(8,128)(2,1)S(1)}, bf16[4,17,8,768]{3,2,1,0:T(8,128)(2,1)S(1)}, u32[]{:S(2)}, u32[]{:S(2)}) collective-permute-start(bf16[4,17,8,768]{3,2,1,0:T(8,128)(2,1)S(1)} %in_order.5.own_ref), channel_id=1, source_target_pairs={{0,4},{4,0},{1,5},{5,1},{2,6},{6,2},{3,7},{7,3},{8,12},{12,8},{9,1... | collective-permute-start | bytes 2506760 | tf_op jit(solution)/shard_map/ppermute | solution.py:68
  47.2 26.6 %collective-permute-start.9 = (bf16[4,17,8,768]{3,2,1,0:T(8,128)(2,1)S(1)}, bf16[4,17,8,768]{3,2,1,0:T(8,128)(2,1)S(1)}, u32[]{:S(2)}, u32[]{:S(2)}) collective-permute-start(bf16[4,17,8,768]{3,2,1,0:T(8,128)(2,1)S(1)} %in_order.5.own_ref), channel_id=1, source_target_pairs={{0,1},{1,0},{2,3},{3,2},{4,5},{5,4},{6,7},{7,6},{8,9},{9,8},{10,11... | collective-permute-start | bytes 2506760 | tf_op jit(solution)/shard_map/ppermute | solution.py:68
  58.6 15.2 %collective-permute-start.7 = (bf16[2,13,8,768]{3,2,1,0:T(8,128)(2,1)S(1)}, bf16[2,13,8,768]{3,2,1,0:T(8,128)(2,1)S(1)}, u32[]{:S(2)}, u32[]{:S(2)}) collective-permute-start(bf16[2,13,8,768]{3,2,1,0:T(8,128)(2,1)S(1)} %slice.92), channel_id=1, source_target_pairs={{0,4},{4,0},{1,5},{5,1},{2,6},{6,2},{3,7},{7,3},{8,12},{12,8},{9,1... | collective-permute-start | bytes 958472 | tf_op jit(solution)/shard_map/ppermute | solution.py:68
  59.2 14.6 %collective-permute-start.8 = (bf16[2,13,8,768]{3,2,1,0:T(8,128)(2,1)S(1)}, bf16[2,13,8,768]{3,2,1,0:T(8,128)(2,1)S(1)}, u32[]{:S(2)}, u32[]{:S(2)}) collective-permute-start(bf16[2,13,8,768]{3,2,1,0:T(8,128)(2,1)S(1)} %slice.93), channel_id=1, source_target_pairs={{0,1},{1,0},{2,3},{3,2},{4,5},{5,4},{6,7},{7,6},{8,9},{9,8},{10,11... | collective-permute-start | bytes 958472 | tf_op jit(solution)/shard_map/ppermute | solution.py:68
  74.6 30.5 %collective-permute-start.16 = (bf16[4,15,8,768]{3,2,1,0:T(8,128)(2,1)S(1)}, bf16[4,15,8,768]{3,2,1,0:T(8,128)(2,1)S(1)}, u32[]{:S(2)}, u32[]{:S(2)}) collective-permute-start(bf16[4,15,8,768]{3,2,1,0:T(8,128)(2,1)S(1)} %in_order.6.own_ref), channel_id=1, source_target_pairs={{0,1},{1,0},{2,3},{3,2},{4,5},{5,4},{6,7},{7,6},{8,9},{9,8},{10,11... | collective-permute-start | bytes 2211848 | tf_op jit(solution)/shard_map/ppermute | solution.py:68
  76.1 29.1 %collective-permute-start.17 = (bf16[4,15,8,768]{3,2,1,0:T(8,128)(2,1)S(1)}, bf16[4,15,8,768]{3,2,1,0:T(8,128)(2,1)S(1)}, u32[]{:S(2)}, u32[]{:S(2)}) collective-permute-start(bf16[4,15,8,768]{3,2,1,0:T(8,128)(2,1)S(1)} %in_order.6.own_ref), channel_id=1, source_target_pairs={{0,4},{4,0},{1,5},{5,1},{2,6},{6,2},{3,7},{7,3},{8,12},{12,8},{9,1... | collective-permute-start | bytes 2211848 | tf_op jit(solution)/shard_map/ppermute | solution.py:68
  77.4 27.7 %collective-permute-start.14 = (bf16[2,17,8,768]{3,2,1,0:T(8,128)(2,1)}, bf16[2,17,8,768]{3,2,1,0:T(8,128)(2,1)}, u32[]{:S(2)}, u32[]{:S(2)}) collective-permute-start(bf16[2,17,8,768]{3,2,1,0:T(8,128)(2,1)} %slice.94), channel_id=1, source_target_pairs={{0,4},{4,0},{1,5},{5,1},{2,6},{6,2},{3,7},{7,3},{8,12},{12,8},{9,1... | collective-permute-start | bytes 1253384 | tf_op jit(solution)/shard_map/ppermute | solution.py:68
  79.7 25.4 %collective-permute-start.15 = (bf16[2,17,8,768]{3,2,1,0:T(8,128)(2,1)}, bf16[2,17,8,768]{3,2,1,0:T(8,128)(2,1)}, u32[]{:S(2)}, u32[]{:S(2)}) collective-permute-start(bf16[2,17,8,768]{3,2,1,0:T(8,128)(2,1)} %slice.95), channel_id=1, source_target_pairs={{0,1},{1,0},{2,3},{3,2},{4,5},{5,4},{6,7},{7,6},{8,9},{9,8},{10,11... | collective-permute-start | bytes 1253384 | tf_op jit(solution)/shard_map/ppermute | solution.py:68
  110.3 25.5 %collective-permute-start.22 = (bf16[4,12,8,768]{3,2,1,0:T(8,128)(2,1)}, bf16[4,12,8,768]{3,2,1,0:T(8,128)(2,1)S(1)}, u32[]{:S(2)}, u32[]{:S(2)}) collective-permute-start(bf16[4,12,8,768]{3,2,1,0:T(8,128)(2,1)} %copy-done.32), channel_id=1, source_target_pairs={{0,1},{1,0},{2,3},{3,2},{4,5},{5,4},{6,7},{7,6},{8,9},{9,8},{10,11... | collective-permute-start | bytes 1769480 | tf_op jit(solution)/shard_map/ppermute | solution.py:68
  111.0 24.9 %collective-permute-start.23 = (bf16[4,12,8,768]{3,2,1,0:T(8,128)(2,1)}, bf16[4,12,8,768]{3,2,1,0:T(8,128)(2,1)S(1)}, u32[]{:S(2)}, u32[]{:S(2)}) collective-permute-start(bf16[4,12,8,768]{3,2,1,0:T(8,128)(2,1)} %copy-done.32), channel_id=1, source_target_pairs={{0,4},{4,0},{1,5},{5,1},{2,6},{6,2},{3,7},{7,3},{8,12},{12,8},{9,1... | collective-permute-start | bytes 1769480 | tf_op jit(solution)/shard_map/ppermute | solution.py:68
  112.5 23.3 %collective-permute-start.20 = (bf16[2,15,8,768]{3,2,1,0:T(8,128)(2,1)S(1)}, bf16[2,15,8,768]{3,2,1,0:T(8,128)(2,1)S(1)}, u32[]{:S(2)}, u32[]{:S(2)}) collective-permute-start(bf16[2,15,8,768]{3,2,1,0:T(8,128)(2,1)S(1)} %slice.97), channel_id=1, source_target_pairs={{0,4},{4,0},{1,5},{5,1},{2,6},{6,2},{3,7},{7,3},{8,12},{12,8},{9,1... | collective-permute-start | bytes 1105928 | tf_op jit(solution)/shard_map/ppermute | solution.py:68
  115.1 20.7 %collective-permute-start.21 = (bf16[2,15,8,768]{3,2,1,0:T(8,128)(2,1)S(1)}, bf16[2,15,8,768]{3,2,1,0:T(8,128)(2,1)S(1)}, u32[]{:S(2)}, u32[]{:S(2)}) collective-permute-start(bf16[2,15,8,768]{3,2,1,0:T(8,128)(2,1)S(1)} %slice.98), channel_id=1, source_target_pairs={{0,1},{1,0},{2,3},{3,2},{4,5},{5,4},{6,7},{7,6},{8,9},{9,8},{10,11... | collective-permute-start | bytes 1105928 | tf_op jit(solution)/shard_map/ppermute | solution.py:68
  179.7 21.3 %collective-permute-start.33 = (bf16[384,768]{1,0:T(8,128)(2,1)S(1)}, bf16[384,768]{1,0:T(8,128)(2,1)S(1)}, u32[]{:S(2)}, u32[]{:S(2)}) collective-permute-start(bf16[384,768]{1,0:T(8,128)(2,1)S(1)} %get-tuple-element.282), channel_id=1, source_target_pairs={{0,1},{1,0},{2,3},{3,2},{4,5},{5,4},{6,7},{7,6},{8,9},{9,8},{10,11... | collective-permute-start | bytes 1769480 | tf_op jit(solution)/shard_map/ppermute | solution.py:68
  180.3 20.7 %collective-permute-start.34 = (bf16[384,768]{1,0:T(8,128)(2,1)S(1)}, bf16[384,768]{1,0:T(8,128)(2,1)S(1)}, u32[]{:S(2)}, u32[]{:S(2)}) collective-permute-start(bf16[384,768]{1,0:T(8,128)(2,1)S(1)} %get-tuple-element.283), channel_id=1, source_target_pairs={{0,4},{4,0},{1,5},{5,1},{2,6},{6,2},{3,7},{7,3},{8,12},{12,8},{9,1... | collective-permute-start | bytes 1769480 | tf_op jit(solution)/shard_map/ppermute | solution.py:68
  182.4 18.6 %collective-permute-start.35 = (bf16[48,3072]{1,0:T(8,128)(2,1)S(1)}, bf16[48,3072]{1,0:T(8,128)(2,1)S(1)}, u32[]{:S(2)}, u32[]{:S(2)}) collective-permute-start(bf16[48,3072]{1,0:T(8,128)(2,1)S(1)} %get-tuple-element.284), channel_id=1, source_target_pairs={{0,4},{4,0},{1,5},{5,1},{2,6},{6,2},{3,7},{7,3},{8,12},{12,8},{9,1... | collective-permute-start | bytes 884744 | tf_op jit(solution)/shard_map/ppermute | solution.py:68
  183.0 18.0 %collective-permute-start.36 = (bf16[48,3072]{1,0:T(8,128)(2,1)S(1)}, bf16[48,3072]{1,0:T(8,128)(2,1)S(1)}, u32[]{:S(2)}, u32[]{:S(2)}) collective-permute-start(bf16[48,3072]{1,0:T(8,128)(2,1)S(1)} %get-tuple-element.285), channel_id=1, source_target_pairs={{0,1},{1,0},{2,3},{3,2},{4,5},{5,4},{6,7},{7,6},{8,9},{9,8},{10,11... | collective-permute-start | bytes 884744 | tf_op jit(solution)/shard_map/ppermute | solution.py:68
  201.2 13.4 %collective-permute-start.37 = (bf16[96,3072]{1,0:T(8,128)(2,1)S(1)}, bf16[96,3072]{1,0:T(8,128)(2,1)S(1)}, u32[]{:S(2)}, u32[]{:S(2)}) collective-permute-start(bf16[96,3072]{1,0:T(8,128)(2,1)S(1)} %get-tuple-element.295), channel_id=1, source_target_pairs={{0,1},{1,0},{2,3},{3,2},{4,5},{5,4},{6,7},{7,6},{8,9},{9,8},{10,11... | collective-permute-start | bytes 1769480 | tf_op jit(solution)/shard_map/ppermute | solution.py:68
  215.8 14.6 %collective-permute-start.40 = (bf16[4,160,3072]{2,1,0:T(8,128)(2,1)S(1)}, bf16[4,160,3072]{2,1,0:T(8,128)(2,1)S(1)}, u32[]{:S(2)}, u32[]{:S(2)}) collective-permute-start(bf16[4,160,3072]{2,1,0:T(8,128)(2,1)S(1)} %get-tuple-element.309), channel_id=1, source_target_pairs={{0,2},{2,0},{1,3},{3,1},{4,6},{6,4},{5,7},{7,5},{8,10},{10,8},{9,1... | collective-permute-start | bytes 11796488 | tf_op jit(solution)/shard_map/ppermute | solution.py:68
  215.9 14.5 %collective-permute-start.42 = (bf16[96,768]{1,0:T(8,128)(2,1)S(1)}, bf16[96,768]{1,0:T(8,128)(2,1)S(1)}, u32[]{:S(2)}, u32[]{:S(2)}) collective-permute-start(bf16[96,768]{1,0:T(8,128)(2,1)S(1)} %get-tuple-element.318), channel_id=1, source_target_pairs={{0,16},{8,24},{16,0},{24,8},{1,17},{9,25},{17,1},{25,9},{2,18},{10... | collective-permute-start | bytes 442376 | tf_op jit(solution)/shard_map/ppermute | solution.py:68
  233.7 15.7 %collective-permute-start.46 = (bf16[4,96,3200]{2,1,0:T(8,128)(2,1)S(1)}, bf16[4,96,3200]{2,1,0:T(8,128)(2,1)S(1)}, u32[]{:S(2)}, u32[]{:S(2)}) collective-permute-start(bf16[4,96,3200]{2,1,0:T(8,128)(2,1)S(1)} %get-tuple-element.340), channel_id=1, source_target_pairs={{0,2},{2,0},{1,3},{3,1},{4,6},{6,4},{5,7},{7,5},{8,10},{10,8},{9,1... | collective-permute-start | bytes 7372808 | tf_op jit(solution)/shard_map/ppermute | solution.py:68
  234.6 13.7 %collective-permute-start.43 = (bf16[80,3072]{1,0:T(8,128)(2,1)S(1)}, bf16[80,3072]{1,0:T(8,128)(2,1)S(1)}, u32[]{:S(2)}, u32[]{:S(2)}) collective-permute-start(bf16[80,3072]{1,0:T(8,128)(2,1)S(1)} %get-tuple-element.328), channel_id=1, source_target_pairs={{0,4},{4,0},{1,5},{5,1},{2,6},{6,2},{3,7},{7,3},{8,12},{12,8},{9,1... | collective-permute-start | bytes 1474568 | tf_op jit(solution)/shard_map/ppermute | solution.py:68
  236.0 13.3 %collective-permute-start.44 = (bf16[80,3072]{1,0:T(8,128)(2,1)S(1)}, bf16[80,3072]{1,0:T(8,128)(2,1)S(1)}, u32[]{:S(2)}, u32[]{:S(2)}) collective-permute-start(bf16[80,3072]{1,0:T(8,128)(2,1)S(1)} %get-tuple-element.329), channel_id=1, source_target_pairs={{0,1},{1,0},{2,3},{3,2},{4,5},{5,4},{6,7},{7,6},{8,9},{9,8},{10,11... | collective-permute-start | bytes 1474568 | tf_op jit(solution)/shard_map/ppermute | solution.py:68
  249.7 31.3 %collective-permute-start.47 = (bf16[160,3072]{1,0:T(8,128)(2,1)S(1)}, bf16[160,3072]{1,0:T(8,128)(2,1)S(1)}, u32[]{:S(2)}, u32[]{:S(2)}) collective-permute-start(bf16[160,3072]{1,0:T(8,128)(2,1)S(1)} %get-tuple-element.345), channel_id=1, source_target_pairs={{0,1},{1,0},{2,3},{3,2},{4,5},{5,4},{6,7},{7,6},{8,9},{9,8},{10,11... | collective-permute-start | bytes 2949128 | tf_op jit(solution)/shard_map/ppermute | solution.py:68
  250.8 30.2 %collective-permute-start.48 = (bf16[160,3072]{1,0:T(8,128)(2,1)S(1)}, bf16[160,3072]{1,0:T(8,128)(2,1)S(1)}, u32[]{:S(2)}, u32[]{:S(2)}) collective-permute-start(bf16[160,3072]{1,0:T(8,128)(2,1)S(1)} %get-tuple-element.346), channel_id=1, source_target_pairs={{0,4},{4,0},{1,5},{5,1},{2,6},{6,2},{3,7},{7,3},{8,12},{12,8},{9,1... | collective-permute-start | bytes 2949128 | tf_op jit(solution)/shard_map/ppermute | solution.py:68
  252.8 27.4 %collective-permute-start.49 = (bf16[48,3200]{1,0:T(8,128)(2,1)S(1)}, bf16[48,3200]{1,0:T(8,128)(2,1)S(1)}, u32[]{:S(2)}, u32[]{:S(2)}) collective-permute-start(bf16[48,3200]{1,0:T(8,128)(2,1)S(1)} %get-tuple-element.349), channel_id=1, source_target_pairs={{0,4},{4,0},{1,5},{5,1},{2,6},{6,2},{3,7},{7,3},{8,12},{12,8},{9,1... | collective-permute-start | bytes 921608 | tf_op jit(solution)/shard_map/ppermute | solution.py:68
  254.2 26.8 %collective-permute-start.50 = (bf16[48,3200]{1,0:T(8,128)(2,1)S(1)}, bf16[48,3200]{1,0:T(8,128)(2,1)S(1)}, u32[]{:S(2)}, u32[]{:S(2)}) collective-permute-start(bf16[48,3200]{1,0:T(8,128)(2,1)S(1)} %get-tuple-element.350), channel_id=1, source_target_pairs={{0,1},{1,0},{2,3},{3,2},{4,5},{5,4},{6,7},{7,6},{8,9},{9,8},{10,11... | collective-permute-start | bytes 921608 | tf_op jit(solution)/shard_map/ppermute | solution.py:68
  255.2 39.7 %collective-permute-start.51 = (bf16[256,768]{1,0:T(8,128)(2,1)S(1)}, bf16[256,768]{1,0:T(8,128)(2,1)S(1)}, u32[]{:S(2)}, u32[]{:S(2)}) collective-permute-start(bf16[256,768]{1,0:T(8,128)(2,1)S(1)} %slice.145), channel_id=1, source_target_pairs={{1,0},{3,2},{5,4},{7,6},{9,8},{11,10},{13,12},{15,14},{17,16},{19,... | collective-permute-start | bytes 1179656 | tf_op jit(solution)/shard_map/ppermute | solution.py:939
  281.2 19.8 %collective-permute-start.54 = (bf16[96,3200]{1,0:T(8,128)(2,1)S(1)}, bf16[96,3200]{1,0:T(8,128)(2,1)S(1)}, u32[]{:S(2)}, u32[]{:S(2)}) collective-permute-start(bf16[96,3200]{1,0:T(8,128)(2,1)S(1)} %get-tuple-element.365), channel_id=1, source_target_pairs={{0,1},{1,0},{2,3},{3,2},{4,5},{5,4},{6,7},{7,6},{8,9},{9,8},{10,11... | collective-permute-start | bytes 1843208 | tf_op jit(solution)/shard_map/ppermute | solution.py:68
  281.4 19.6 %collective-permute-start.55 = (bf16[96,3200]{1,0:T(8,128)(2,1)S(1)}, bf16[96,3200]{1,0:T(8,128)(2,1)S(1)}, u32[]{:S(2)}, u32[]{:S(2)}) collective-permute-start(bf16[96,3200]{1,0:T(8,128)(2,1)S(1)} %get-tuple-element.366), channel_id=1, source_target_pairs={{0,4},{4,0},{1,5},{5,1},{2,6},{6,2},{3,7},{7,3},{8,12},{12,8},{9,1... | collective-permute-start | bytes 1843208 | tf_op jit(solution)/shard_map/ppermute | solution.py:68
  (108 other events, 770.8 us)
